TPU v7x, 1024 devices: a whole 4x8x16 slice. The times are simulated.
1024 devices in a mesh: gx: 256 (over y, z, core), gy: 4 (over x).
Axes of the slice: x: 4, y: 8, z: 16, core: 2. Of those that a mesh axis runs over, the one named last changes fastest.
Arguments:
- rhs: float32 [256, 8, 4, 1024], P('gx', 'gy'), may hold values from -4 to 4
- blocks: float32 [256, 8, 4, 7, 4096], P('gx', 'gy'), may hold values from -0.5 to 0.5
Outputs:
- basis_out: float32 [5, 256, 8, 4, 1024], P(None, 'gx', 'gy')
- factor_out: float32 [80, 80], replicated
All inputs are finite; a program needn't handle non-finite values.
Results may differ from a plain program's by a relative error of at most 0.0003.
Values sent between devices are 32-bit elements; how exact they have to be, the bound alone decides.
A program may use at most 32 MiB of HBM per device.

v0:
```python
import jax
import jax.numpy as jnp
from jax import lax
from jax.sharding import PartitionSpec as P

DOF = 64
RHS = 16
POWERS = 4
COLS = 80


precise = lax.Precision.HIGHEST


def extended(block, sides, width):
    for axis, dim in sides:
        count = lax.axis_size(axis)
        forward = [(i, i + 1) for i in range(count - 1)]
        backward = [(target, source) for source, target in forward]
        low = lax.ppermute(
            lax.slice_in_dim(block, block.shape[dim] - width, None, axis=dim), axis, forward
        )
        high = lax.ppermute(lax.slice_in_dim(block, 0, width, axis=dim), axis, backward)
        block = jnp.concatenate([low, block, high], axis=dim)
    return block


def couple(matrices, neighbour, face):
    return jnp.einsum("abcij,abcjr->abcir", matrices[:, :, :, face], neighbour, precision=precise)


def ghosted(vector):
    cells_x, cells_y, cells_z = (vector.shape[0], vector.shape[1], vector.shape[2])
    flat_vector = vector.reshape(cells_x, cells_y, cells_z, DOF * RHS)
    padded = extended(flat_vector, (("gx", 0), ("gy", 1)), 1)
    return padded.reshape(cells_x + 2, cells_y + 2, cells_z, DOF, RHS)


def apply_operator(matrices, vector):
    zpadded = jnp.pad(vector, ((0, 0), (0, 0), (1, 1), (0, 0), (0, 0)))
    padded = ghosted(vector)
    neighbours = [
        vector,
        padded[:-2, 1:-1],
        padded[2:, 1:-1],
        padded[1:-1, :-2],
        padded[1:-1, 2:],
        zpadded[:, :, :-2],
        zpadded[:, :, 2:],
    ]
    summed = vector
    for face in range(7):
        summed = summed + couple(matrices, neighbours[face], face)
    return summed


def upper_factor(gram_matrix):
    order = gram_matrix.shape[0]
    index_rows = lax.broadcasted_iota(jnp.int32, (order,), 0)
    index_cols = lax.broadcasted_iota(jnp.int32, (order, order), 1)

    def one_column(column, carry):
        remain, lower = carry
        column_vec = lax.dynamic_slice_in_dim(remain, column, 1, 1)[:, 0]
        pivot = jnp.sqrt(lax.dynamic_slice_in_dim(column_vec, column, 1, 0)[0])
        scaled = jnp.where(index_rows >= column, column_vec / pivot, jnp.zeros_like(column_vec))
        lower = jnp.where(index_cols == column, scaled[:, None], lower)
        remain = remain - scaled[:, None] * scaled[None, :]
        return (remain, lower)

    start = (gram_matrix, jnp.zeros_like(gram_matrix))
    remain, lower = lax.fori_loop(0, order, one_column, start)
    return lower.T


def upper_inverse(factor):
    order = factor.shape[0]
    index_rows = lax.broadcasted_iota(jnp.int32, (order, order), 0)
    index_vec = lax.broadcasted_iota(jnp.int32, (order,), 0)

    def one_row(step, solved):
        row = order - 1 - step
        factor_row = lax.dynamic_slice_in_dim(factor, row, 1, 0)[0]
        pivot = lax.dynamic_slice_in_dim(factor_row, row, 1, 0)[0]
        unit_row = jnp.where(
            index_vec == row, jnp.ones_like(factor_row), jnp.zeros_like(factor_row)
        )
        new_row = (unit_row - jnp.dot(factor_row, solved, precision=precise)) / pivot
        return jnp.where(index_rows == row, new_row[None, :], solved)

    return lax.fori_loop(0, order, one_row, jnp.zeros_like(factor))


def global_factor(krylov):
    gram_local = jnp.einsum("kxr,lxs->krls", krylov, krylov, precision=precise).reshape(COLS, COLS)
    return upper_factor(lax.psum(gram_local, ("gx", "gy")))


def apply_inverse(krylov, factor):
    inverse = upper_inverse(factor)
    return jnp.einsum(
        "lxs,lskr->kxr",
        krylov,
        inverse.reshape(POWERS + 1, RHS, POWERS + 1, RHS),
        precision=precise,
    )


def on_device(rhs, blocks):
    cells_x, cells_y, cells_z = (rhs.shape[0], rhs.shape[1], rhs.shape[2])
    matrices = blocks.reshape(cells_x, cells_y, cells_z, 7, DOF, DOF)
    vector = rhs.reshape(cells_x, cells_y, cells_z, DOF, RHS)
    collected = [vector]
    for power_index in range(POWERS):
        vector = apply_operator(matrices, vector)
        collected.append(vector)
    krylov = jnp.stack(collected).reshape(POWERS + 1, cells_x * cells_y * cells_z * DOF, RHS)
    first_r = global_factor(krylov)
    first_q = apply_inverse(krylov, first_r)
    second_r = global_factor(first_q)
    second_q = apply_inverse(first_q, second_r)
    basis_out = second_q.reshape(POWERS + 1, cells_x, cells_y, cells_z, DOF * RHS)
    factor_out = jnp.dot(second_r, first_r, precision=precise)
    return (basis_out, factor_out)


def solution(mesh):
    return jax.shard_map(
        on_device,
        mesh=mesh,
        in_specs=(P("gx", "gy", None, None), P("gx", "gy", None, None, None)),
        out_specs=(P(None, "gx", "gy", None, None), P()),
        check_vma=False,
    )
```

profile of v0, /device:TPU:1, one launch (start us, length us, event | category | flops | bytes accessed | tf_op | source)
XLA Modules:
  0.0 1037.2 jit_solution(2926751132637669467)
XLA Ops:
  0.6 5.4 collective-permute-start
  6.0 12.0 %collective-permute-start.1 = (f32[1,2,4,1024]{3,2,1,0:T(4,128)}, f32[1,2,4,1024]{3,2,1,0:T(4,128)S(1)}, u32[]{:S(2)}, u32[]{:S(2)}) collective-permute-start(f32[1,2,4,1024]{3,2,1,0:T(4,128)} %param.10), channel_id=1, source_target_pairs={{4,0},{8,4},{12,8},{16,12},{20,16},{24,20},{28,24},{32,28},{36,32}... | collective-permute-start | bytes 98312 | tf_op jit(solution)/shard_map/ppermute | solution.py:23
  28.1 3.4 collective-permute-done.3
  32.2 1.5 reshape.358
  37.7 1.9 collective-permute-start.4
  39.6 2.4 collective-permute-start.5
  43.3 1.5 collective-permute-done.5
  48.2 2.9 collective-permute-done.7
  51.9 1.5 reshape.373
  57.0 3.3 collective-permute-start.8
  60.4 1.9 collective-permute-start.9
  63.6 2.0 collective-permute-done.9
  65.6 1.6 collective-permute-start.10
  67.3 1.5 collective-permute-start.11
  69.4 2.7 collective-permute-done.11
  72.8 1.5 reshape.381
  78.1 3.3 collective-permute-start.12
  81.4 1.9 collective-permute-start.13
  84.6 2.0 collective-permute-done.13
  86.7 1.6 collective-permute-start.14
  90.2 2.9 collective-permute-done.15
  93.9 1.5 reshape.389
  100.9 135.6 %psum.14 = f32[80,80]{1,0:T(8,128)S(1)} all-reduce(f32[80,80]{1,0:T(8,128)S(1)} %fusion.101), channel_id=1, replica_groups=mesh['gx'=256,'gy'=4] {'gx','gy'}, use_global_device_ids=true, to_apply=%region_0.1 | all-reduce | flops 6400 | bytes 51200 | tf_op jit(solution)/shard_map/psum | solution.py:96
  236.5 222.1 %while.72 = (s32[]{:T(128)}, f32[80,80]{0,1:T(8,128)S(1)}, f32[80,80]{0,1:T(8,128)}, s32[]{:T(128)}, s32[]{:T(128)}, /*index=5*/s32[]{:T(128)}) while((s32[]{:T(128)}, f32[80,80]{0,1:T(8,128)S(1)}, f32[80,80]{0,1:T(8,128)}, s32[]{:T(128)}, s32[]{:T(128)}, /*index=5*/s32[]{:T(128)}) %tuple.181), condition=%wide.region_2.3_spmd.clone, body=%wide.region_1.2_spmd.clone.sunk | while | flops 32404 | bytes 106299 | solution.py:72
  458.6 229.2 %while.73 = (s32[]{:T(128)}, f32[80,80]{1,0:T(8,128)S(1)}, f32[80,80]{1,0:T(8,128)}, s32[]{:T(128)}, s32[]{:T(128)}, /*index=5*/s32[]{:T(128)}, s32[]{:T(128)}) while((s32[]{:T(128)}, f32[80,80]{1,0:T(8,128)S(1)}, f32[80,80]{1,0:T(8,128)}, s32[]{:T(128)}, s32[]{:T(128)}, /*index=5*/s32[]{:T(128)}, s32[]{:T(128)}) %tuple.195), condition=%wide.region_4.5_spmd.clone, body=%wide.region_3.4_spmd.clone.sunk | while | flops 102728 | bytes 78638 | solution.py:91
  460.0 1.5 fusion.124
  462.9 1.5 fusion.124
  465.7 1.5 fusion.124
  471.4 1.5 fusion.124
  474.3 1.5 fusion.124
  477.2 1.5 fusion.124
  480.0 1.5 fusion.124
  482.9 1.5 fusion.124
  485.8 1.5 fusion.124
  491.5 1.5 fusion.124
  494.4 1.5 fusion.124
  497.2 1.5 fusion.124
  500.1 1.5 fusion.124
  503.0 1.5 fusion.124
  508.7 1.5 fusion.124
  511.6 1.5 fusion.124
  514.4 1.5 fusion.124
  517.3 1.5 fusion.124
  520.1 1.5 fusion.124
  525.9 1.5 fusion.124
  528.7 1.5 fusion.124
  531.6 1.5 fusion.124
  534.5 1.5 fusion.124
  537.3 1.5 fusion.124
  540.2 1.5 fusion.124
  545.9 1.5 fusion.124
  548.8 1.5 fusion.124
  551.7 1.5 fusion.124
  554.5 1.5 fusion.124
  557.4 1.5 fusion.124
  563.1 1.5 fusion.124
  566.0 1.5 fusion.124
  568.9 1.5 fusion.124
  571.7 1.5 fusion.124
  574.6 1.5 fusion.124
  580.3 1.5 fusion.124
  689.5 118.1 %psum.15 = f32[80,80]{1,0:T(8,128)S(1)} all-reduce(f32[80,80]{1,0:T(8,128)S(1)} %reshape.397), channel_id=1, replica_groups=mesh['gx'=256,'gy'=4] {'gx','gy'}, use_global_device_ids=true, to_apply=%region_5.6 | all-reduce | flops 6400 | bytes 51200 | tf_op jit(solution)/shard_map/psum | solution.py:96
  807.6 111.8 %while.74 = (s32[]{:T(128)}, f32[80,80]{0,1:T(8,128)S(1)}, f32[80,80]{0,1:T(8,128)S(1)}, s32[]{:T(128)}, s32[]{:T(128)}, /*index=5*/s32[]{:T(128)}) while((s32[]{:T(128)}, f32[80,80]{0,1:T(8,128)S(1)}, f32[80,80]{0,1:T(8,128)S(1)}, s32[]{:T(128)}, s32[]{:T(128)}, /*index=5*/s32[]{:T(128)}) %tuple.193), condition=%wide.region_7.8_spmd.clone, body=%wide.region_6.7_spmd.clone.sunk | while | flops 32404 | bytes 106299 | solution.py:72
  920.2 114.5 %while.75 = (s32[]{:T(128)}, f32[80,80]{1,0:T(8,128)S(1)}, f32[80,80]{1,0:T(8,128)S(1)}, s32[]{:T(128)}, s32[]{:T(128)}, /*index=5*/s32[]{:T(128)}, s32[]{:T(128)}) while((s32[]{:T(128)}, f32[80,80]{1,0:T(8,128)S(1)}, f32[80,80]{1,0:T(8,128)S(1)}, s32[]{:T(128)}, s32[]{:T(128)}, /*index=5*/s32[]{:T(128)}, s32[]{:T(128)}) %tuple.194), condition=%wide.region_9.10_spmd.clone, body=%wide.region_8.9_spmd.clone.sunk | while | flops 102728 | bytes 93490 | solution.py:91
  (1212 shorter events, 550.4 us)
Async XLA Ops:
  0.6 24.1 %collective-permute-start = (f32[1,2,4,1024]{3,2,1,0:T(4,128)}, f32[1,2,4,1024]{3,2,1,0:T(4,128)S(1)}, u32[]{:S(2)}, u32[]{:S(2)}) collective-permute-start(f32[1,2,4,1024]{3,2,1,0:T(4,128)} %param.10), channel_id=1, source_target_pairs={{0,4},{4,8},{8,12},{12,16},{16,20},{20,24},{24,28},{28,32},{32,36}... | collective-permute-start | bytes 98312 | tf_op jit(solution)/shard_map/ppermute | solution.py:20
  6.0 18.8 %collective-permute-start.1 = (f32[1,2,4,1024]{3,2,1,0:T(4,128)}, f32[1,2,4,1024]{3,2,1,0:T(4,128)S(1)}, u32[]{:S(2)}, u32[]{:S(2)}) collective-permute-start(f32[1,2,4,1024]{3,2,1,0:T(4,128)} %param.10), channel_id=1, source_target_pairs={{4,0},{8,4},{12,8},{16,12},{20,16},{24,20},{28,24},{32,28},{36,32}... | collective-permute-start | bytes 98312 | tf_op jit(solution)/shard_map/ppermute | solution.py:23
  21.0 3.5 copy-start.6
  24.9 3.2 collective-permute-start.2
  26.2 5.3 collective-permute-start.3
  33.7 3.2 copy-start.7
  37.7 5.6 collective-permute-start.4
  39.6 5.2 collective-permute-start.5
  44.9 3.3 collective-permute-start.6
  46.3 4.8 collective-permute-start.7
  53.3 2.9 copy-start.9
  56.7 15.4 %copy-start = (f32[2,4,64,16]{2,3,1,0:T(8,128)}, f32[2,4,64,16]{2,3,1,0:T(8,128)S(1)}, u32[]{:S(2)}) copy-start(f32[2,4,64,16]{2,3,1,0:T(8,128)S(1)} %fusion.48) | copy-start | bytes 98308
  57.0 6.5 collective-permute-start.8
  60.4 5.2 collective-permute-start.9
  65.6 3.8 collective-permute-start.10
  67.3 4.8 collective-permute-start.11
  72.8 3.8 copy-start.1
  74.4 2.9 copy-start.2
  74.4 2.9 copy-start.10
  78.1 6.5 collective-permute-start.12
  81.4 5.2 collective-permute-start.13
  86.7 3.6 collective-permute-start.14
  88.3 4.8 collective-permute-start.15
  95.4 2.9 copy-start.8
  99.5 588.4 %copy-start.3 = (f32[5,512,16]{1,2,0:T(8,128)S(1)}, f32[5,512,16]{1,2,0:T(8,128)}, u32[]{:S(2)}) copy-start(f32[5,512,16]{1,2,0:T(8,128)} %constant_dynamic-update-slice_fusion.12) | copy-start | bytes 491524
  458.6 349.0 %copy-start.4 = (f32[80,80]{0,1:T(8,128)S(1)}, f32[80,80]{0,1:T(8,128)}, u32[]{:S(2)}) copy-start(f32[80,80]{0,1:T(8,128)} %custom-call.2) | copy-start | bytes 76804
  687.8 231.6 %copy-start.5 = (f32[80,80]{1,0:T(8,128)S(1)}, f32[80,80]{1,0:T(8,128)}, u32[]{:S(2)}) copy-start(f32[80,80]{1,0:T(8,128)} %get-tuple-element.889) | copy-start | bytes 76804
where the time goes:
time: 1050 us; the launch traced here: 1040 us
  local copies, waits for them, and re-layouts  271 us (26%)
  blocking collectives  254 us (24%)
  matrix products  203 us (19%)
  other arithmetic  128 us (12%)
  loops' own time  119 us (11%)
  starting transfers between devices  43.5 us (4%)
  waiting for transfers between devices  17.6 us (2%)
    psum x2, blocking collectives, global_factor(): return upper_factor(lax.psum(gram_local, ('gx', 'gy')))  254 us
    dot_general x160, matrix products, one_row(): jnp.dot(factor_row, solved, precision=precise)  180 us
    dynamic_slice x160, local copies, waits for them, and re-layouts, one_row(): pivot = lax.dynamic_slice_in_dim(factor_row, row, 1, 0)[0]  155 us
    select_n x160, other arithmetic, one_column(): lower = jnp.where(index_cols == column, scaled[:, None], lower)  119 us
    another operation x2, loops' own time, upper_factor(): remain, lower = lax.fori_loop(0, order, one_column, start)  113 us
    dynamic_slice x160, local copies, waits for them, and re-layouts, one_column(): pivot = jnp.sqrt(lax.dynamic_slice_in_dim(column_vec, column, 1, 0)[0])  98.8 us
    ppermute x8, starting transfers between devices, extended(): lax.ppermute(lax.slice_in_dim(block, 0, width, axis=dim), axis, backward)  23.6 us
  transfers between devices with their start and end apart: 16, of which 7 were waited for; matrix products, arithmetic and copies ran while one was open for 1% of the time, Pallas kernels for 0%

commit v1 on v0

v1 whole, which is shorter than its diff:
```python
import functools

import jax
import jax.numpy as jnp
from jax import lax
from jax.experimental import pallas as pl
from jax.experimental.pallas import tpu as pltpu
from jax.sharding import PartitionSpec as P

DOF = 64
RHS = 16
POWERS = 4
COLS = 80
ELEMS = 8
LANES = 128
F32 = jnp.float32
BF16 = jnp.bfloat16
PAIRS = ((0, 5), (6, None), (1, 2), (3, 4))


def lane(shape):
    return lax.broadcasted_iota(jnp.int32, shape, len(shape) - 1)


def row(shape):
    return lax.broadcasted_iota(jnp.int32, shape, 0)


def split(a):
    high = a.astype(BF16)
    rest = a - high.astype(F32)
    mid = rest.astype(BF16)
    low = (rest - mid.astype(F32)).astype(BF16)
    return high, mid, low


def dot(a, b, dims=((1,), (0,))):
    return lax.dot_general(a, b, (dims, ((), ())), preferred_element_type=F32)


def dot_exact(a, b, dims=((1,), (0,))):
    return lax.dot_general(
        a, b, (dims, ((), ())), precision=lax.Precision.HIGHEST, preferred_element_type=F32
    )


def transpose_groups(a):
    rows, group = row(a.shape) % 8, lane(a.shape) // 16
    count = a.shape[0]
    for bit in (1, 2, 4):
        up = pltpu.roll(pltpu.roll(a, bit, 0), LANES - 16 * bit, 1)
        down = pltpu.roll(pltpu.roll(a, count - bit, 0), 16 * bit, 1)
        r, g = (rows // bit) % 2, (group // bit) % 2
        a = jnp.where(r == g, a, jnp.where(r == 1, up, down))
    return a


def transpose_arrays(arrays):
    group = lane((DOF, LANES)) // 16
    arrays = list(arrays)
    for bit in (1, 2, 4):
        g = (group // bit) % 2
        out = []
        for place in range(8):
            other = arrays[place ^ bit]
            here = arrays[place]
            if (place // bit) % 2:
                out.append(jnp.where(g == 1, here, pltpu.roll(other, LANES - 16 * bit, 1)))
            else:
                out.append(jnp.where(g == 0, here, pltpu.roll(other, 16 * bit, 1)))
        arrays = out
    return arrays


def bcast_lane(a, index):
    return jnp.broadcast_to(a[:, index : index + 1], (8, LANES))


def bcast_row(a, index):
    return jnp.broadcast_to(a[index : index + 1, :], (8, LANES))


def eliminate(a_ref, w_ref):
    tiles = COLS // 8

    def panel(p, _):
        start = pl.multiple_of(8 * p, 8)
        shift = lax.rem(LANES - 8 * p, LANES)
        a_p, w_p = a_ref[pl.ds(start, 8), :], w_ref[pl.ds(start, 8), :]
        near = pltpu.roll(a_p, shift, 1)
        column = [bcast_lane(near, j) for j in range(8)]
        a = [[bcast_row(column[j], m) for j in range(m + 1)] for m in range(8)]
        inv = [None] * 8
        for j in range(8):
            inv[j] = lax.rsqrt(a[j][j])
            for m in range(j + 1, 8):
                a[m][j] = a[m][j] * inv[j]
            for m in range(j + 1, 8):
                for n in range(j + 1, m + 1):
                    a[m][n] = a[m][n] - a[m][j] * a[n][j]
        li = [[None] * 8 for _ in range(8)]
        for j in range(8):
            li[j][j] = inv[j]
            for i in range(j + 1, 8):
                total = a[i][j] * li[j][j]
                for k in range(j + 1, i):
                    total = total + a[i][k] * li[k][j]
                li[i][j] = -inv[i] * total

        def apply(vectors):
            out = []
            for m in range(8):
                total = li[m][0] * vectors[0]
                for j in range(1, m + 1):
                    total = total + li[m][j] * vectors[j]
                out.append(total)
            return out

        r = apply([bcast_row(a_p, j) for j in range(8)])
        w = apply([bcast_row(w_p, j) for j in range(8)])
        for i in range(tiles):
            a_i, w_i = a_ref[8 * i : 8 * i + 8, :], w_ref[8 * i : 8 * i + 8, :]
            at = pltpu.roll(a_i, shift, 1)
            c = apply([bcast_lane(at, j) for j in range(8)])
            a_n, w_n = a_i, w_i
            for m in range(8):
                a_n = a_n - c[m] * r[m]
                w_n = w_n - c[m] * w[m]
            later = i > p
            a_ref[8 * i : 8 * i + 8, :] = jnp.where(later, a_n, a_i)
            w_ref[8 * i : 8 * i + 8, :] = jnp.where(later, w_n, w_i)
        rows = row((8, LANES))
        r_p, w_q = r[0], w[0]
        for m in range(1, 8):
            r_p = jnp.where(rows == m, r[m], r_p)
            w_q = jnp.where(rows == m, w[m], w_q)
        a_ref[pl.ds(start, 8), :] = jnp.where(lane((8, LANES)) >= rows + start, r_p, 0.0)
        w_ref[pl.ds(start, 8), :] = w_q
        return 0

    lax.fori_loop(0, tiles, panel, 0)


def kernel(sizes, rhs_ref, blocks_ref, basis_ref, factor_ref, raw, flat, b_f32, b_parts, vecs, ypack, hx, hy,
           u_ref, packed, stage_a, stage_b, stage_c, sum_a, sum_b, sum_c, gathered, a_ref, w_ref, r_ref,
           load_sem, hsend, hrecv, asend, arecv):
    ny, nz, nc, nx = sizes
    gx, gy = ny * nz * nc, nx
    me_x, me_y = lax.axis_index("gx"), lax.axis_index("gy")
    core, chip = lax.rem(me_x, nc), lax.div(me_x, nc)
    at_z, at_y = lax.rem(chip, nz), lax.div(chip, nz)

    def place(y, z, c, x):
        return {"gx": (y * nz + z) * nc + c, "gy": x}

    me_g = me_y * nc + core
    n_g = nx * nc

    def mate_g(i):
        return place(at_y, at_z, lax.rem(i, nc), lax.div(i, nc))

    def mate_y(i):
        return place(i, at_z, core, me_y)

    def mate_z(i):
        return place(at_y, i, core, me_y)

    groups = ((n_g, me_g, mate_g), (ny, at_y, mate_y), (nz, at_z, mate_z))
    near = (
        {"gx": lax.rem(me_x + gx - 1, gx), "gy": me_y},
        {"gx": lax.rem(me_x + 1, gx), "gy": me_y},
        {"gx": me_x, "gy": lax.rem(me_y + gy - 1, gy)},
        {"gx": me_x, "gy": lax.rem(me_y + 1, gy)},
    )

    loads = [
        pltpu.make_async_copy(rhs_ref, flat, load_sem.at[0]),
        pltpu.make_async_copy(blocks_ref, raw, load_sem.at[1]),
    ]
    for load in loads:
        load.start()
    barrier = pltpu.get_barrier_semaphore()
    count = 0
    for peer in near:
        pl.semaphore_signal(barrier, inc=1, device_id=peer, device_id_type=pl.DeviceIdType.MESH)
        count += 1
    for n, me, mate in groups:

        @pl.loop(1, n)
        def _(d):
            pl.semaphore_signal(
                barrier, inc=1, device_id=mate(lax.rem(me + d, n)), device_id_type=pl.DeviceIdType.MESH
            )

        count += n - 1

    loads[0].wait()
    flat_rhs = jnp.concatenate([flat[0], flat[1]], axis=0)
    first = jnp.concatenate([flat_rhs[:, LANES * t : LANES * (t + 1)] for t in range(8)], axis=0)
    lanes = lane((DOF, LANES))
    half = lane((DOF // 2, LANES)) < 64

    def remote(src, dst, send, recv, peer):
        return pltpu.make_async_remote_copy(
            src_ref=src, dst_ref=dst, send_sem=send, recv_sem=recv,
            device_id=peer, device_id_type=pl.DeviceIdType.MESH,
        )

    def exchanges(k):
        return (
            remote(vecs.at[k], hx.at[k, 1], hsend.at[k, 0], hrecv.at[k, 0], near[0]),
            remote(vecs.at[k], hx.at[k, 0], hsend.at[k, 1], hrecv.at[k, 1], near[1]),
            remote(ypack.at[k, 0], hy.at[k, 1], hsend.at[k, 2], hrecv.at[k, 2], near[2]),
            remote(ypack.at[k, 1], hy.at[k, 0], hsend.at[k, 3], hrecv.at[k, 3], near[3]),
        )

    def publish(k, v):
        vecs[k] = v
        low, high = v[: DOF // 2], pltpu.roll(v[DOF // 2 :], 64, 1)
        ypack[k, 0] = jnp.where(half, low, high)
        ypack[k, 1] = jnp.where(half, high, low)

    v = transpose_groups(first)
    publish(0, v)
    pl.semaphore_wait(barrier, count)
    sends = [exchanges(0)]
    for copy in sends[0]:
        copy.start()

    loads[1].wait()
    zero8 = jnp.zeros((8, LANES), F32)
    half8 = lane((8, LANES)) < 64

    @pl.loop(0, DOF // 2)
    def _(t):
        at = pl.multiple_of(t * LANES, LANES)

        def face(f):
            if f is None:
                return zero8
            return jnp.concatenate([raw[f, :, pl.ds(at, LANES)], raw[7 + f, :, pl.ds(at, LANES)]], axis=0)

        for place_, (one, two) in enumerate(PAIRS):
            a, b = face(one), face(two)
            b_f32[place_, pl.ds(2 * t, 8, stride=DOF), :] = jnp.where(half8, a, pltpu.roll(b, 64, 1))
            b_f32[place_, pl.ds(2 * t + 1, 8, stride=DOF), :] = jnp.where(half8, pltpu.roll(a, 64, 1), b)

    for place_ in range(4):
        for part, value in enumerate(split(b_f32[place_])):
            b_parts[part, :, LANES * place_ : LANES * (place_ + 1)] = value

    def product(place_, vectors):
        high, mid, low = split(jnp.concatenate(vectors, axis=0))
        both = jnp.concatenate([high, mid], axis=1)
        columns = slice(256 * place_, 256 * (place_ + 1))
        b_high, b_mid, b_low = (b_parts[part, :, columns] for part in range(3))
        wide = dot(b_high, both) + dot(b_mid, both)
        return wide[:, :LANES] + wide[:, LANES:] + (dot(b_high, low) + dot(b_low, high))

    def of_element(a):
        out = jnp.zeros((DOF, LANES), F32)
        for e in range(ELEMS):
            out = jnp.where(lanes // 16 == e, a[DOF * e : DOF * (e + 1)], out)
        return out

    at_cell = (lanes // 16) % 4
    zero = jnp.zeros((DOF, LANES), F32)
    for k in range(POWERS):
        z_low = jnp.where(at_cell == 0, 0.0, pltpu.roll(v, 16, 1))
        z_high = jnp.where(at_cell == 3, 0.0, pltpu.roll(v, LANES - 16, 1))
        inner = product(0, [v, z_low, z_high, zero])
        swapped = pltpu.roll(v, 64, 1)
        for copy in sends[k]:
            copy.wait_recv()
        x_low = jnp.where(me_x > 0, hx[k, 0], 0.0)
        x_high = jnp.where(me_x < gx - 1, hx[k, 1], 0.0)
        y_low = jnp.where(me_y > 0, hy[k, 0], 0.0)
        y_high = jnp.where(me_y < gy - 1, hy[k, 1], 0.0)
        own_low, own_high = swapped[: DOF // 2], swapped[DOF // 2 :]
        y_low = jnp.concatenate(
            [jnp.where(half, pltpu.roll(y_low, 64, 1), own_low), jnp.where(half, y_low, own_high)], axis=0
        )
        y_high = jnp.concatenate(
            [jnp.where(half, own_low, pltpu.roll(y_high, 64, 1)), jnp.where(half, own_high, y_high)], axis=0
        )
        outer = product(1, [x_low, x_high, y_low, y_high])
        v = v + of_element(inner + outer)
        if k < POWERS - 1:
            publish(k + 1, v)
            sends.append(exchanges(k + 1))
            for copy in sends[k + 1]:
                copy.start()
        else:
            vecs[POWERS] = v

    columns = transpose_arrays([vecs[k] for k in range(POWERS + 1)] + [zero] * (7 - POWERS))
    for e in range(ELEMS):
        u_ref[DOF * e : DOF * (e + 1), :] = columns[e]

    def all_bytes(buffer, n, sem):
        return pltpu.make_async_copy(buffer.at[pl.ds(0, n - 1)], buffer.at[pl.ds(0, n - 1)], sem)

    def add_up(buffer, n):
        total = buffer[0]
        for i in range(1, n):
            total = total + buffer[i]
        return total

    def one_pass(number, _):
        u = u_ref[...]
        gram = dot_exact(u, u, ((0,), (0,)))[:COLS]
        def block(k, to):
            part = gram[RHS * k : RHS * (k + 1)]
            return pltpu.roll(part, (to - RHS * k) % LANES, 1) if (to - RHS * k) % LANES else part

        lane16 = lane((RHS, LANES))
        top = jnp.where(lane16 < 80, block(0, 0), block(2, 80))
        low = jnp.where(lane16 < 64, block(1, 0), jnp.where(lane16 < 96, block(3, 64), block(4, 96)))
        both = jnp.concatenate([top, low], axis=0)
        piece = 2 * RHS // n_g
        for i in range(n_g):
            packed[number, i] = both[piece * i : piece * (i + 1)]

        def start_all(n, me, mate, src, dst, sem):
            @pl.loop(1, n)
            def _(d):
                other = lax.rem(me + d, n)
                remote(src(other), dst, asend.at[number, sem], arecv.at[number, sem], mate(other)).start()

        start_all(n_g, me_g, mate_g, lambda i: packed.at[number, i], stage_a.at[number, me_g], 0)
        stage_a[number, me_g] = packed[number, me_g]
        all_bytes(stage_a.at[number], n_g, arecv.at[number, 0]).wait()
        sum_a[number] = add_up(stage_a.at[number], n_g)
        start_all(ny, at_y, mate_y, lambda i: sum_a.at[number], stage_b.at[number, at_y], 1)
        stage_b[number, at_y] = sum_a[number]
        all_bytes(stage_b.at[number], ny, arecv.at[number, 1]).wait()
        sum_b[number] = add_up(stage_b.at[number], ny)
        start_all(nz, at_z, mate_z, lambda i: sum_b.at[number], stage_c.at[number, at_z], 2)
        stage_c[number, at_z] = sum_b[number]
        all_bytes(stage_c.at[number], nz, arecv.at[number, 2]).wait()
        sum_c[number] = add_up(stage_c.at[number], nz)
        start_all(n_g, me_g, mate_g, lambda i: sum_c.at[number], gathered.at[number, me_g], 3)
        gathered[number, me_g] = sum_c[number]
        all_bytes(gathered.at[number], n_g, arecv.at[number, 3]).wait()

        both = jnp.concatenate([gathered[number, i] for i in range(n_g)], axis=0)
        top, low = both[:RHS], both[RHS:]
        blocks_of = (
            (top, 0, 80), (low, 0, 64), (top, 80, 48), (low, 64, 32), (low, 96, 16)
        )
        upper = []
        for k, (source, at, width) in enumerate(blocks_of):
            shift = (RHS * k - at) % LANES
            part = pltpu.roll(source, shift, 1) if shift else source
            upper.append(jnp.where((lane16 >= RHS * k) & (lane16 < COLS), part, 0.0))
        upper = jnp.concatenate(upper + [jnp.zeros((LANES - COLS, LANES), F32)], axis=0)
        r_, c_ = row((LANES, LANES)), lane((LANES, LANES))
        full = jnp.where(r_ // RHS <= c_ // RHS, upper, upper.T)
        a_ref[...] = full[:COLS]
        w_ref[...] = (r_ == c_).astype(F32)[:COLS]
        eliminate(a_ref, w_ref)
        r_ref[number] = a_ref[...]
        inverse = jnp.concatenate([w_ref[...], jnp.zeros((LANES - COLS, LANES), F32)], axis=0)
        u_ref[...] = dot_exact(u, inverse, ((1,), (1,)))
        return 0

    lax.fori_loop(0, 2, one_pass, 0)

    pad = jnp.zeros((LANES - COLS, LANES), F32)
    factor = dot_exact(r_ref[1], jnp.concatenate([r_ref[0], pad], axis=0))
    factor_ref[...] = factor[:, :COLS]
    columns = transpose_arrays([u_ref[DOF * e : DOF * (e + 1), :] for e in range(ELEMS)])
    for k in range(POWERS + 1):
        out = transpose_groups(columns[k])
        for t in range(8):
            at = slice(LANES * t, LANES * (t + 1))
            basis_ref[k, 0, :, at] = out[8 * t : 8 * t + 4]
            basis_ref[k, 1, :, at] = out[8 * t + 4 : 8 * t + 8]

    for copies in sends:
        for copy in copies:
            copy.wait_send()
    for number in range(2):
        all_bytes(stage_a.at[number], n_g, asend.at[number, 0]).wait()
        all_bytes(stage_b.at[number], ny, asend.at[number, 1]).wait()
        all_bytes(stage_c.at[number], nz, asend.at[number, 2]).wait()
        all_bytes(gathered.at[number], n_g, asend.at[number, 3]).wait()


def on_device(sizes, rhs, blocks):
    ny, nz, nc, nx = sizes
    n_g = nx * nc
    piece = 2 * RHS // n_g
    faces = blocks.transpose(0, 1, 3, 2, 4).reshape(14, 4, DOF * DOF)
    vmem = pltpu.VMEM
    basis, factor = pl.pallas_call(
        functools.partial(kernel, sizes),
        out_shape=(
            jax.ShapeDtypeStruct((POWERS + 1, 2, 4, DOF * RHS), F32),
            jax.ShapeDtypeStruct((COLS, COLS), F32),
        ),
        in_specs=[pl.BlockSpec(memory_space=pl.ANY)] * 2,
        out_specs=(pl.BlockSpec(memory_space=pltpu.VMEM),) * 2,
        scratch_shapes=[
            vmem((14, 4, DOF * DOF), F32),
            vmem((2, 4, DOF * RHS), F32),
            vmem((4, ELEMS * DOF, LANES), F32),
            vmem((3, ELEMS * DOF, 4 * LANES), BF16),
            vmem((POWERS + 1, DOF, LANES), F32),
            vmem((POWERS, 2, DOF // 2, LANES), F32),
            vmem((POWERS, 2, DOF, LANES), F32),
            vmem((POWERS, 2, DOF // 2, LANES), F32),
            vmem((ELEMS * DOF, LANES), F32),
            vmem((2, n_g, piece, LANES), F32),
            vmem((2, n_g, piece, LANES), F32),
            vmem((2, ny, piece, LANES), F32),
            vmem((2, nz, piece, LANES), F32),
            vmem((2, piece, LANES), F32),
            vmem((2, piece, LANES), F32),
            vmem((2, piece, LANES), F32),
            vmem((2, n_g, piece, LANES), F32),
            vmem((COLS, LANES), F32),
            vmem((COLS, LANES), F32),
            vmem((2, COLS, LANES), F32),
            pltpu.SemaphoreType.DMA((2,)),
            pltpu.SemaphoreType.DMA((POWERS, 4)),
            pltpu.SemaphoreType.DMA((POWERS, 4)),
            pltpu.SemaphoreType.DMA((2, 4)),
            pltpu.SemaphoreType.DMA((2, 4)),
        ],
        compiler_params=pltpu.CompilerParams(
            collective_id=0, has_side_effects=True, vmem_limit_bytes=40 * 1024 * 1024
        ),
        name="krylov_qr",
    )(rhs.reshape(2, 4, DOF * RHS), faces)
    return basis.reshape(POWERS + 1, 1, 2, 4, DOF * RHS), factor


def solution(mesh):
    gx, gy = mesh.shape["gx"], mesh.shape["gy"]
    nz = 16 if gx >= 64 else 2
    return jax.shard_map(
        functools.partial(on_device, (gx // (2 * nz), nz, 2, gy)),
        mesh=mesh,
        in_specs=(P("gx", "gy", None, None), P("gx", "gy", None, None, None)),
        out_specs=(P(None, "gx", "gy", None, None), P()),
        check_vma=False,
    )
```

time: 1050 us -> 97 us (0.09); the launches traced: 1040 us -> 96.8 us
  local copies, waits for them, and re-layouts: 271 us -> 3.22 us
  blocking collectives: 254 us -> 0 us
  matrix products: 203 us -> 0 us
  other arithmetic: 128 us -> 0 us
  loops' own time: 119 us -> 0 us
  Pallas kernels: 0 us -> 92.9 us
  starting transfers between devices: 43.5 us -> 0 us
  waiting for transfers between devices: 17.6 us -> 0 us
    psum x2 -> x0, blocking collectives: 254 us -> none  [global_factor(): return upper_factor(lax.psum(gram_local, ('gx', 'gy')))]
    dynamic_slice x320 -> x0, local copies, waits for them, and re-layouts: 253 us -> none  [the longest x160 155 us: one_row(): pivot = lax.dynamic_slice_in_dim(factor_row, row, 1, 0)[0]]
    dot_general x193 -> x0, matrix products: 203 us -> none  [the longest x160 180 us: one_row(): jnp.dot(factor_row, solved, precision=precise)]
    select_n x480 -> x0, other arithmetic: 123 us -> none  [the longest x160 119 us: one_column(): lower = jnp.where(index_cols == column, scaled[:, None], lower)]
    another operation x4 -> x0, loops' own time: 119 us -> none  [the longest x2 113 us: upper_factor(): remain, lower = lax.fori_loop(0, order, one_column, start)]
    pallas_call x0 -> x1, Pallas kernels: none -> 92.9 us  [on_device(): pl.pallas_call(functools.partial(kernel, sizes), out_shape=(jax.ShapeDtyp...]
    ppermute x16 -> x0, starting transfers between devices: 43.5 us -> none  [the longest x8 23.6 us: extended(): lax.ppermute(lax.slice_in_dim(block, 0, width, axis=dim), axis, backward)]
    ppermute x16 -> x0, waiting for transfers between devices: 17.6 us -> none  [the longest x8 17.5 us: extended(): lax.ppermute(lax.slice_in_dim(block, 0, width, axis=dim), axis, backward)]
  transfers between devices with their start and end apart: 16 -> 0, of which waited for: 7 -> 0; matrix products, arithmetic and copies ran while one was open for 1% -> 0% of each run, Pallas kernels for 0% -> 0%
where the time goes in v1:
time: 97 us; the launch traced here: 96.8 us
  Pallas kernels  92.9 us (96%)
  local copies, waits for them, and re-layouts  3.22 us (3%)
    pallas_call x1, Pallas kernels, on_device(): pl.pallas_call(functools.partial(kernel, sizes), out_shape=(jax.ShapeDtyp...  92.9 us
    unnamed x6, local copies, waits for them, and re-layouts  3.22 us

profile of v1, /device:TPU:1, one launch (start us, length us, event | category | flops | bytes accessed | tf_op | source)
XLA Modules:
  0.0 96.8 jit_solution(15129325836726030306)
XLA Ops:
  0.6 0.0 copy-start
  0.6 1.2 %copy-done = f32[1,2,4,7,4096]{4,2,3,1,0:T(4,128)S(1)} copy-done((f32[1,2,4,7,4096]{4,2,3,1,0:T(4,128)S(1)}, f32[1,2,4,7,4096]{4,2,3,1,0:T(4,128)}, u32[]{:S(2)}) %copy-start) | copy-done | bytes 917528
  1.8 0.0 copy-start.1
  1.8 0.8 copy-done.1
  2.6 92.9 %krylov_qr.1 = (f32[5,2,4,1024]{3,2,1,0:T(4,128)S(1)}, f32[80,80]{1,0:T(8,128)S(1)}) custom-call(f32[2,4,1024]{2,1,0:T(4,128)S(1)} %bitcast.9, f32[14,4,4096]{2,1,0:T(4,128)S(1)} %bitcast.7), custom_call_target="tpu_custom_call" | custom-call | tf_op jit(solution)/shard_map/krylov_qr/pallas_call | solution.py:396
  95.5 0.7 copy.7
  96.1 0.6 copy.8
Async XLA Ops:
  0.6 1.2 %copy-start = (f32[1,2,4,7,4096]{4,2,3,1,0:T(4,128)S(1)}, f32[1,2,4,7,4096]{4,2,3,1,0:T(4,128)}, u32[]{:S(2)}) copy-start(f32[1,2,4,7,4096]{4,2,3,1,0:T(4,128)} %param.3) | copy-start | bytes 2752516
  1.8 0.8 copy-start.1

commit v2 on v1

--- a/solution.py
+++ b/solution.py
@@ -72,78 +72,57 @@
     return arrays
 
 
-def bcast_lane(a, index):
-    return jnp.broadcast_to(a[:, index : index + 1], (8, LANES))
-
-
-def bcast_row(a, index):
-    return jnp.broadcast_to(a[index : index + 1, :], (8, LANES))
-
-
-def eliminate(a_ref, w_ref):
-    tiles = COLS // 8
-
-    def panel(p, _):
-        start = pl.multiple_of(8 * p, 8)
-        shift = lax.rem(LANES - 8 * p, LANES)
-        a_p, w_p = a_ref[pl.ds(start, 8), :], w_ref[pl.ds(start, 8), :]
-        near = pltpu.roll(a_p, shift, 1)
-        column = [bcast_lane(near, j) for j in range(8)]
-        a = [[bcast_row(column[j], m) for j in range(m + 1)] for m in range(8)]
-        inv = [None] * 8
+def pick(a, index):
+    return a[index : index + 1, :]
+
+
+def spread(a, index):
+    return jnp.broadcast_to(a[:, index : index + 1], a.shape)
+
+
+def stacked(rows):
+    at = row((8, LANES))
+    out = jnp.broadcast_to(rows[0], (8, LANES))
+    for m in range(1, 8):
+        out = jnp.where(at == m, rows[m], out)
+    return out
+
+
+def eliminate(full):
+    later = full
+    rest = (row((COLS, LANES)) == lane((COLS, LANES))).astype(F32)
+    factor, inverse = [], []
+    for p in range(COLS // 8):
+        start = 8 * p
+        at, at_w = later[:8], rest[:8]
+        later, rest = later[8:], rest[8:]
+        more = p < COLS // 8 - 1
+        column = [spread(at, start + j) for j in range(8)]
+        r, w = [pick(at, j) for j in range(8)], [pick(at_w, j) for j in range(8)]
+        below = [spread(later, start + j) for j in range(8)] if more else None
         for j in range(8):
-            inv[j] = lax.rsqrt(a[j][j])
+            inv = lax.rsqrt(pick(column[j], j))
+            r[j], w[j] = r[j] * inv, w[j] * inv
+            scaled = column[j] * inv
             for m in range(j + 1, 8):
-                a[m][j] = a[m][j] * inv[j]
-            for m in range(j + 1, 8):
-                for n in range(j + 1, m + 1):
-                    a[m][n] = a[m][n] - a[m][j] * a[n][j]
-        li = [[None] * 8 for _ in range(8)]
-        for j in range(8):
-            li[j][j] = inv[j]
-            for i in range(j + 1, 8):
-                total = a[i][j] * li[j][j]
-                for k in range(j + 1, i):
-                    total = total + a[i][k] * li[k][j]
-                li[i][j] = -inv[i] * total
-
-        def apply(vectors):
-            out = []
-            for m in range(8):
-                total = li[m][0] * vectors[0]
-                for j in range(1, m + 1):
-                    total = total + li[m][j] * vectors[j]
-                out.append(total)
-            return out
-
-        r = apply([bcast_row(a_p, j) for j in range(8)])
-        w = apply([bcast_row(w_p, j) for j in range(8)])
-        for i in range(tiles):
-            a_i, w_i = a_ref[8 * i : 8 * i + 8, :], w_ref[8 * i : 8 * i + 8, :]
-            at = pltpu.roll(a_i, shift, 1)
-            c = apply([bcast_lane(at, j) for j in range(8)])
-            a_n, w_n = a_i, w_i
-            for m in range(8):
-                a_n = a_n - c[m] * r[m]
-                w_n = w_n - c[m] * w[m]
-            later = i > p
-            a_ref[8 * i : 8 * i + 8, :] = jnp.where(later, a_n, a_i)
-            w_ref[8 * i : 8 * i + 8, :] = jnp.where(later, w_n, w_i)
-        rows = row((8, LANES))
-        r_p, w_q = r[0], w[0]
-        for m in range(1, 8):
-            r_p = jnp.where(rows == m, r[m], r_p)
-            w_q = jnp.where(rows == m, w[m], w_q)
-        a_ref[pl.ds(start, 8), :] = jnp.where(lane((8, LANES)) >= rows + start, r_p, 0.0)
-        w_ref[pl.ds(start, 8), :] = w_q
-        return 0
-
-    lax.fori_loop(0, tiles, panel, 0)
+                s = pick(scaled, m)
+                column[m] = column[m] - scaled * s
+                r[m], w[m] = r[m] - s * r[j], w[m] - s * w[j]
+            if more:
+                below[j] = below[j] * inv
+                for m in range(j + 1, 8):
+                    below[m] = below[m] - below[j] * pick(scaled, m)
+                later = later - below[j] * r[j]
+                rest = rest - below[j] * w[j]
+        upper = lane((8, LANES)) >= row((8, LANES)) + start
+        factor.append(jnp.where(upper, stacked(r), 0.0))
+        inverse.append(stacked(w))
+    return jnp.concatenate(factor, axis=0), jnp.concatenate(inverse, axis=0)
 
 
 def kernel(sizes, rhs_ref, blocks_ref, basis_ref, factor_ref, raw, flat, b_f32, b_parts, vecs, ypack, hx, hy,
-           u_ref, packed, stage_a, stage_b, stage_c, sum_a, sum_b, sum_c, gathered, a_ref, w_ref, r_ref,
-           load_sem, hsend, hrecv, asend, arecv):
+           u_ref, packed, stage_a, stage_b, stage_c, sum_a, sum_b, sum_c, gathered, r_ref,
+           load_sem, hsend, hrecv, asend, arecv, word):
     ny, nz, nc, nx = sizes
     gx, gy = ny * nz * nc, nx
     me_x, me_y = lax.axis_index("gx"), lax.axis_index("gy")
@@ -180,19 +159,23 @@
     for load in loads:
         load.start()
     barrier = pltpu.get_barrier_semaphore()
-    count = 0
-    for peer in near:
-        pl.semaphore_signal(barrier, inc=1, device_id=peer, device_id_type=pl.DeviceIdType.MESH)
-        count += 1
-    for n, me, mate in groups:
-
-        @pl.loop(1, n)
-        def _(d):
-            pl.semaphore_signal(
-                barrier, inc=1, device_id=mate(lax.rem(me + d, n)), device_id_type=pl.DeviceIdType.MESH
-            )
-
-        count += n - 1
+
+    def signal(semaphore, peer):
+        pl.semaphore_signal(semaphore, inc=1, device_id=peer, device_id_type=pl.DeviceIdType.MESH)
+
+    def at_distance(d):
+        peers = []
+        for n, me, mate in groups[1:]:
+            if d == 1 or 2 * d <= n // 2:
+                peers += [mate(lax.rem(me + d, n)), mate(lax.rem(me + n - d, n))]
+        return peers
+
+    greeted = list(near) + at_distance(1)
+    for peer in greeted:
+        signal(barrier, peer)
+    for d in range(1, n_g):
+        signal(barrier, mate_g(lax.rem(me_g + d, n_g)))
+    count = len(greeted) + n_g - 1
 
     loads[0].wait()
     flat_rhs = jnp.concatenate([flat[0], flat[1]], axis=0)
@@ -220,56 +203,65 @@
         ypack[k, 0] = jnp.where(half, low, high)
         ypack[k, 1] = jnp.where(half, high, low)
 
+    zero8 = jnp.zeros((8, LANES), F32)
+    half8 = lane((8, LANES)) < 64
+
+    def prepare(places):
+        @pl.loop(0, DOF // 8)
+        def _(quad):
+            for step in range(4):
+                t = 4 * quad + step
+                at = pl.multiple_of(t * LANES, LANES)
+
+                def face(f):
+                    if f is None:
+                        return zero8
+                    return jnp.concatenate([raw[f, :, pl.ds(at, LANES)], raw[7 + f, :, pl.ds(at, LANES)]], axis=0)
+
+                for place_ in places:
+                    one, two = PAIRS[place_]
+                    a, b = face(one), face(two)
+                    b_f32[place_, pl.ds(2 * t, 8, stride=DOF), :] = jnp.where(half8, a, pltpu.roll(b, 64, 1))
+                    b_f32[place_, pl.ds(2 * t + 1, 8, stride=DOF), :] = jnp.where(half8, pltpu.roll(a, 64, 1), b)
+
+        for i, place_ in enumerate(places):
+            high, mid, low = split(b_f32[place_])
+            for part, value in enumerate((mid, high, low)):
+                at = 2 * LANES * part + LANES * i
+                b_parts[places[0] // 2, :, at : at + LANES] = value
+
     v = transpose_groups(first)
     publish(0, v)
+    loads[1].wait()
+    prepare((0, 1))
     pl.semaphore_wait(barrier, count)
     sends = [exchanges(0)]
     for copy in sends[0]:
         copy.start()
-
-    loads[1].wait()
-    zero8 = jnp.zeros((8, LANES), F32)
-    half8 = lane((8, LANES)) < 64
-
-    @pl.loop(0, DOF // 2)
-    def _(t):
-        at = pl.multiple_of(t * LANES, LANES)
-
-        def face(f):
-            if f is None:
-                return zero8
-            return jnp.concatenate([raw[f, :, pl.ds(at, LANES)], raw[7 + f, :, pl.ds(at, LANES)]], axis=0)
-
-        for place_, (one, two) in enumerate(PAIRS):
-            a, b = face(one), face(two)
-            b_f32[place_, pl.ds(2 * t, 8, stride=DOF), :] = jnp.where(half8, a, pltpu.roll(b, 64, 1))
-            b_f32[place_, pl.ds(2 * t + 1, 8, stride=DOF), :] = jnp.where(half8, pltpu.roll(a, 64, 1), b)
-
-    for place_ in range(4):
-        for part, value in enumerate(split(b_f32[place_])):
-            b_parts[part, :, LANES * place_ : LANES * (place_ + 1)] = value
-
-    def product(place_, vectors):
+    prepare((2, 3))
+
+    def product(which, vectors):
         high, mid, low = split(jnp.concatenate(vectors, axis=0))
         both = jnp.concatenate([high, mid], axis=1)
-        columns = slice(256 * place_, 256 * (place_ + 1))
-        b_high, b_mid, b_low = (b_parts[part, :, columns] for part in range(3))
-        wide = dot(b_high, both) + dot(b_mid, both)
-        return wide[:, :LANES] + wide[:, LANES:] + (dot(b_high, low) + dot(b_low, high))
-
-    def of_element(a):
-        out = jnp.zeros((DOF, LANES), F32)
-        for e in range(ELEMS):
-            out = jnp.where(lanes // 16 == e, a[DOF * e : DOF * (e + 1)], out)
+        wide = dot(b_parts[which, :, : 4 * LANES], jnp.concatenate([both, both], axis=0))
+        rest = dot(b_parts[which, :, 2 * LANES :], jnp.concatenate([low, high], axis=0))
+        total = wide[:, :LANES] + wide[:, LANES:] + rest
+        out = total[:DOF]
+        for e in range(1, ELEMS):
+            out = jnp.where(lanes // 16 == e, total[DOF * e : DOF * (e + 1)], out)
         return out
 
+    known = [at_distance(d) for d in (1, 2, 4) if 2 * d <= max(ny, nz) // 2]
     at_cell = (lanes // 16) % 4
     zero = jnp.zeros((DOF, LANES), F32)
     for k in range(POWERS):
         z_low = jnp.where(at_cell == 0, 0.0, pltpu.roll(v, 16, 1))
         z_high = jnp.where(at_cell == 3, 0.0, pltpu.roll(v, LANES - 16, 1))
-        inner = product(0, [v, z_low, z_high, zero])
+        inner = v + product(0, [v, z_low, z_high, zero])
         swapped = pltpu.roll(v, 64, 1)
+        if k < len(known):
+            for peer in known[k]:
+                signal(word.at[k], peer)
         for copy in sends[k]:
             copy.wait_recv()
         x_low = jnp.where(me_x > 0, hx[k, 0], 0.0)
@@ -284,7 +276,9 @@
             [jnp.where(half, own_low, pltpu.roll(y_high, 64, 1)), jnp.where(half, own_high, y_high)], axis=0
         )
         outer = product(1, [x_low, x_high, y_low, y_high])
-        v = v + of_element(inner + outer)
+        if k < len(known):
+            pl.semaphore_wait(word.at[k], len(known[k]))
+        v = inner + outer
         if k < POWERS - 1:
             publish(k + 1, v)
             sends.append(exchanges(k + 1))
@@ -322,8 +316,7 @@
             packed[number, i] = both[piece * i : piece * (i + 1)]
 
         def start_all(n, me, mate, src, dst, sem):
-            @pl.loop(1, n)
-            def _(d):
+            for d in sorted(range(1, n), key=lambda d: -min(d, n - d)):
                 other = lax.rem(me + d, n)
                 remote(src(other), dst, asend.at[number, sem], arecv.at[number, sem], mate(other)).start()
 
@@ -356,11 +349,9 @@
         upper = jnp.concatenate(upper + [jnp.zeros((LANES - COLS, LANES), F32)], axis=0)
         r_, c_ = row((LANES, LANES)), lane((LANES, LANES))
         full = jnp.where(r_ // RHS <= c_ // RHS, upper, upper.T)
-        a_ref[...] = full[:COLS]
-        w_ref[...] = (r_ == c_).astype(F32)[:COLS]
-        eliminate(a_ref, w_ref)
-        r_ref[number] = a_ref[...]
-        inverse = jnp.concatenate([w_ref[...], jnp.zeros((LANES - COLS, LANES), F32)], axis=0)
+        factor, inverse = eliminate(full[:COLS])
+        r_ref[number] = factor
+        inverse = jnp.concatenate([inverse, jnp.zeros((LANES - COLS, LANES), F32)], axis=0)
         u_ref[...] = dot_exact(u, inverse, ((1,), (1,)))
         return 0
 
@@ -405,7 +396,7 @@
             vmem((14, 4, DOF * DOF), F32),
             vmem((2, 4, DOF * RHS), F32),
             vmem((4, ELEMS * DOF, LANES), F32),
-            vmem((3, ELEMS * DOF, 4 * LANES), BF16),
+            vmem((2, ELEMS * DOF, 6 * LANES), BF16),
             vmem((POWERS + 1, DOF, LANES), F32),
             vmem((POWERS, 2, DOF // 2, LANES), F32),
             vmem((POWERS, 2, DOF, LANES), F32),
@@ -419,17 +410,16 @@
             vmem((2, piece, LANES), F32),
             vmem((2, piece, LANES), F32),
             vmem((2, n_g, piece, LANES), F32),
-            vmem((COLS, LANES), F32),
-            vmem((COLS, LANES), F32),
             vmem((2, COLS, LANES), F32),
             pltpu.SemaphoreType.DMA((2,)),
             pltpu.SemaphoreType.DMA((POWERS, 4)),
             pltpu.SemaphoreType.DMA((POWERS, 4)),
             pltpu.SemaphoreType.DMA((2, 4)),
             pltpu.SemaphoreType.DMA((2, 4)),
+            pltpu.SemaphoreType.REGULAR((POWERS,)),
         ],
         compiler_params=pltpu.CompilerParams(
-            collective_id=0, has_side_effects=True, vmem_limit_bytes=40 * 1024 * 1024
+            collective_id=0, has_side_effects=True, vmem_limit_bytes=60 * 1024 * 1024
         ),
         name="krylov_qr",
     )(rhs.reshape(2, 4, DOF * RHS), faces)

time: 97 us -> 87.8 us (0.905)
  Pallas kernels: 92.9 us -> 84.7 us
  local copies, waits for them, and re-layouts: 3.22 us -> 2.22 us
    pallas_call x1, Pallas kernels: 92.9 us -> 84.7 us  [on_device(): pl.pallas_call(functools.partial(kernel, sizes), out_shape=(jax.ShapeDtyp...]
    unnamed x6 -> x4, local copies, waits for them, and re-layouts: 3.22 us -> 2.22 us
where the time goes in v2:
time: 87.8 us; the launch traced here: 87.6 us
  Pallas kernels  84.7 us (96%)
  local copies, waits for them, and re-layouts  2.22 us (3%)
    pallas_call x1, Pallas kernels, on_device(): pl.pallas_call(functools.partial(kernel, sizes), out_shape=(jax.ShapeDtyp...  84.7 us
    unnamed x4, local copies, waits for them, and re-layouts  2.22 us

profile of v2, /device:TPU:1, one launch (start us, length us, event | category | flops | bytes accessed | tf_op | source)
XLA Modules:
  0.0 87.6 jit_solution(13921206002879733311)
XLA Ops:
  0.6 84.7 %krylov_qr.1 = (f32[5,2,4,1024]{3,2,1,0:T(4,128)}, f32[80,80]{1,0:T(8,128)}) custom-call(f32[2,4,1024]{2,1,0:T(4,128)} %bitcast.9, f32[14,4,4096]{2,1,0:T(4,128)} %bitcast.7), custom_call_target="tpu_custom_call" | custom-call | tf_op jit(solution)/shard_map/krylov_qr/pallas_call | solution.py:387
  85.4 0.0 copy-start
  85.4 1.6 %copy.7 = f32[5,1,2,4,1024]{4,3,2,1,0:T(4,128)} copy(f32[5,1,2,4,1024]{4,3,2,1,0:T(4,128)} %bitcast.8) | data formatting | bytes 327680
  87.0 0.0 copy-done
  87.0 0.6 copy.8
Async XLA Ops:
  85.4 1.6 %copy-start = (f32[80,80]{1,0:T(8,128)S(1)}, f32[80,80]{1,0:T(8,128)}, u32[]{:S(2)}) copy-start(f32[80,80]{1,0:T(8,128)} %get-tuple-element.11) | copy-start | bytes 76804

commit v3 on v2

--- a/solution.py
+++ b/solution.py
@@ -13,6 +13,7 @@
 COLS = 80
 ELEMS = 8
 LANES = 128
+PANEL = 16
 F32 = jnp.float32
 BF16 = jnp.bfloat16
 PAIRS = ((0, 5), (6, None), (1, 2), (3, 4))
@@ -38,10 +39,15 @@
     return lax.dot_general(a, b, (dims, ((), ())), preferred_element_type=F32)
 
 
-def dot_exact(a, b, dims=((1,), (0,))):
-    return lax.dot_general(
-        a, b, (dims, ((), ())), precision=lax.Precision.HIGHEST, preferred_element_type=F32
-    )
+def dot_exact(a, b, side=1):
+    a_high, a_mid, a_low = split(a)
+    b_high, b_mid, b_low = split(b)
+    both = jnp.concatenate([b_high, b_mid], axis=1)
+    dims = ((side,), (0,))
+    wide = dot(jnp.concatenate([a_mid, a_high], axis=side), jnp.concatenate([both, both], axis=0), dims)
+    rest = dot(jnp.concatenate([a_high, a_low], axis=side), jnp.concatenate([b_low, b_high], axis=0), dims)
+    n = b.shape[1]
+    return wide[:, :n] + wide[:, n:] + rest
 
 
 def transpose_groups(a):
@@ -81,46 +87,51 @@
 
 
 def stacked(rows):
-    at = row((8, LANES))
-    out = jnp.broadcast_to(rows[0], (8, LANES))
-    for m in range(1, 8):
+    at = row((PANEL, LANES))
+    out = jnp.broadcast_to(rows[0], (PANEL, LANES))
+    for m in range(1, PANEL):
         out = jnp.where(at == m, rows[m], out)
     return out
 
 
 def eliminate(full):
     later = full
-    rest = (row((COLS, LANES)) == lane((COLS, LANES))).astype(F32)
-    factor, inverse = [], []
-    for p in range(COLS // 8):
-        start = 8 * p
-        at, at_w = later[:8], rest[:8]
-        later, rest = later[8:], rest[8:]
-        more = p < COLS // 8 - 1
-        column = [spread(at, start + j) for j in range(8)]
-        r, w = [pick(at, j) for j in range(8)], [pick(at_w, j) for j in range(8)]
-        below = [spread(later, start + j) for j in range(8)] if more else None
-        for j in range(8):
+    upper, diagonal, inverse = [], [], []
+    for p in range(COLS // PANEL):
+        start = PANEL * p
+        more = p < COLS // PANEL - 1
+        column = [spread(later[:PANEL], start + j) for j in range(PANEL)]
+        below = [spread(later[PANEL:], start + j) for j in range(PANEL)] if more else None
+        at = lane(later.shape)
+        own = (at >= start) & (at < start + PANEL)
+        later = jnp.where(own, (row(later.shape) + start == at).astype(F32), later)
+        first, later = later[:PANEL], later[PANEL:]
+        r = [pick(first, j) for j in range(PANEL)]
+        at = lane((PANEL, LANES))
+        corner = jnp.zeros((PANEL, LANES), F32)
+        for j in range(PANEL):
             inv = lax.rsqrt(pick(column[j], j))
-            r[j], w[j] = r[j] * inv, w[j] * inv
+            r[j] = r[j] * inv
             scaled = column[j] * inv
-            for m in range(j + 1, 8):
+            corner = jnp.where(at == start + j, scaled, corner)
+            for m in range(j + 1, PANEL):
                 s = pick(scaled, m)
                 column[m] = column[m] - scaled * s
-                r[m], w[m] = r[m] - s * r[j], w[m] - s * w[j]
+                r[m] = r[m] - s * r[j]
             if more:
                 below[j] = below[j] * inv
-                for m in range(j + 1, 8):
+                for m in range(j + 1, PANEL):
                     below[m] = below[m] - below[j] * pick(scaled, m)
                 later = later - below[j] * r[j]
-                rest = rest - below[j] * w[j]
-        upper = lane((8, LANES)) >= row((8, LANES)) + start
-        factor.append(jnp.where(upper, stacked(r), 0.0))
-        inverse.append(stacked(w))
-    return jnp.concatenate(factor, axis=0), jnp.concatenate(inverse, axis=0)
-
-
-def kernel(sizes, rhs_ref, blocks_ref, basis_ref, factor_ref, raw, flat, b_f32, b_parts, vecs, ypack, hx, hy,
+        rows = stacked(r)
+        inverse.append(jnp.where(at < start + PANEL, rows, 0.0))
+        upper.append(jnp.where(at >= start + PANEL, rows, 0.0))
+        diagonal.append(jnp.where(at <= row((PANEL, LANES)) + start, corner, 0.0))
+    below = jnp.concatenate(diagonal + [jnp.zeros((LANES - COLS, LANES), F32)], axis=0)
+    return jnp.concatenate(upper, axis=0) + below.T[:COLS], jnp.concatenate(inverse, axis=0)
+
+
+def kernel(sizes, rhs_ref, blocks_ref, basis_ref, factor_ref, raw, b_f32, b_parts, vecs, ypack, hx, hy,
            u_ref, packed, stage_a, stage_b, stage_c, sum_a, sum_b, sum_c, gathered, r_ref,
            load_sem, hsend, hrecv, asend, arecv, word):
     ny, nz, nc, nx = sizes
@@ -152,12 +163,8 @@
         {"gx": me_x, "gy": lax.rem(me_y + 1, gy)},
     )
 
-    loads = [
-        pltpu.make_async_copy(rhs_ref, flat, load_sem.at[0]),
-        pltpu.make_async_copy(blocks_ref, raw, load_sem.at[1]),
-    ]
-    for load in loads:
-        load.start()
+    load = pltpu.make_async_copy(blocks_ref, raw, load_sem.at[0])
+    load.start()
     barrier = pltpu.get_barrier_semaphore()
 
     def signal(semaphore, peer):
@@ -177,8 +184,7 @@
         signal(barrier, mate_g(lax.rem(me_g + d, n_g)))
     count = len(greeted) + n_g - 1
 
-    loads[0].wait()
-    flat_rhs = jnp.concatenate([flat[0], flat[1]], axis=0)
+    flat_rhs = jnp.concatenate([rhs_ref[0], rhs_ref[1]], axis=0)
     first = jnp.concatenate([flat_rhs[:, LANES * t : LANES * (t + 1)] for t in range(8)], axis=0)
     lanes = lane((DOF, LANES))
     half = lane((DOF // 2, LANES)) < 64
@@ -198,10 +204,16 @@
         )
 
     def publish(k, v):
+        copies = exchanges(k)
         vecs[k] = v
+        for copy in copies[:2]:
+            copy.start()
         low, high = v[: DOF // 2], pltpu.roll(v[DOF // 2 :], 64, 1)
         ypack[k, 0] = jnp.where(half, low, high)
         ypack[k, 1] = jnp.where(half, high, low)
+        for copy in copies[2:]:
+            copy.start()
+        return copies
 
     zero8 = jnp.zeros((8, LANES), F32)
     half8 = lane((8, LANES)) < 64
@@ -231,13 +243,10 @@
                 b_parts[places[0] // 2, :, at : at + LANES] = value
 
     v = transpose_groups(first)
-    publish(0, v)
-    loads[1].wait()
+    pl.semaphore_wait(barrier, count)
+    sends = [publish(0, v)]
+    load.wait()
     prepare((0, 1))
-    pl.semaphore_wait(barrier, count)
-    sends = [exchanges(0)]
-    for copy in sends[0]:
-        copy.start()
     prepare((2, 3))
 
     def product(which, vectors):
@@ -280,10 +289,7 @@
             pl.semaphore_wait(word.at[k], len(known[k]))
         v = inner + outer
         if k < POWERS - 1:
-            publish(k + 1, v)
-            sends.append(exchanges(k + 1))
-            for copy in sends[k + 1]:
-                copy.start()
+            sends.append(publish(k + 1, v))
         else:
             vecs[POWERS] = v
 
@@ -302,7 +308,7 @@
 
     def one_pass(number, _):
         u = u_ref[...]
-        gram = dot_exact(u, u, ((0,), (0,)))[:COLS]
+        gram = dot_exact(u, u, 0)[:COLS]
         def block(k, to):
             part = gram[RHS * k : RHS * (k + 1)]
             return pltpu.roll(part, (to - RHS * k) % LANES, 1) if (to - RHS * k) % LANES else part
@@ -352,7 +358,7 @@
         factor, inverse = eliminate(full[:COLS])
         r_ref[number] = factor
         inverse = jnp.concatenate([inverse, jnp.zeros((LANES - COLS, LANES), F32)], axis=0)
-        u_ref[...] = dot_exact(u, inverse, ((1,), (1,)))
+        u_ref[...] = dot_exact(u, inverse.T)
         return 0
 
     lax.fori_loop(0, 2, one_pass, 0)
@@ -390,11 +396,10 @@
             jax.ShapeDtypeStruct((POWERS + 1, 2, 4, DOF * RHS), F32),
             jax.ShapeDtypeStruct((COLS, COLS), F32),
         ),
-        in_specs=[pl.BlockSpec(memory_space=pl.ANY)] * 2,
+        in_specs=[pl.BlockSpec(memory_space=pltpu.VMEM), pl.BlockSpec(memory_space=pl.ANY)],
         out_specs=(pl.BlockSpec(memory_space=pltpu.VMEM),) * 2,
         scratch_shapes=[
             vmem((14, 4, DOF * DOF), F32),
-            vmem((2, 4, DOF * RHS), F32),
             vmem((4, ELEMS * DOF, LANES), F32),
             vmem((2, ELEMS * DOF, 6 * LANES), BF16),
             vmem((POWERS + 1, DOF, LANES), F32),
@@ -411,7 +416,7 @@
             vmem((2, piece, LANES), F32),
             vmem((2, n_g, piece, LANES), F32),
             vmem((2, COLS, LANES), F32),
-            pltpu.SemaphoreType.DMA((2,)),
+            pltpu.SemaphoreType.DMA((1,)),
             pltpu.SemaphoreType.DMA((POWERS, 4)),
             pltpu.SemaphoreType.DMA((POWERS, 4)),
             pltpu.SemaphoreType.DMA((2, 4)),
@@ -419,7 +424,7 @@
             pltpu.SemaphoreType.REGULAR((POWERS,)),
         ],
         compiler_params=pltpu.CompilerParams(
-            collective_id=0, has_side_effects=True, vmem_limit_bytes=60 * 1024 * 1024
+            collective_id=0, has_side_effects=True, vmem_limit_bytes=53 * 1024 * 1024 + 256 * 1024
         ),
         name="krylov_qr",
     )(rhs.reshape(2, 4, DOF * RHS), faces)

time: 87.8 us -> 85.9 us (0.978)
  Pallas kernels: 84.7 us -> 83 us
    pallas_call x1, Pallas kernels: 84.7 us -> 83 us  [on_device(): pl.pallas_call(functools.partial(kernel, sizes), out_shape=(jax.ShapeDtyp...]
where the time goes in v3:
time: 85.9 us; the launch traced here: 85.7 us
  Pallas kernels  83 us (97%)
  local copies, waits for them, and re-layouts  2.04 us (2%)
    pallas_call x1, Pallas kernels, on_device(): pl.pallas_call(functools.partial(kernel, sizes), out_shape=(jax.ShapeDtyp...  83 us
    unnamed x4, local copies, waits for them, and re-layouts  2.04 us

profile of v3, /device:TPU:1, one launch (start us, length us, event | category | flops | bytes accessed | tf_op | source)
XLA Modules:
  0.0 85.7 jit_solution(837034681034895734)
XLA Ops:
  0.6 0.0 copy-start
  0.6 0.7 copy-done
  1.4 83.0 %krylov_qr.1 = (f32[5,2,4,1024]{3,2,1,0:T(4,128)S(1)}, f32[80,80]{1,0:T(8,128)S(1)}) custom-call(f32[2,4,1024]{2,1,0:T(4,128)S(1)} %bitcast.8, f32[14,4,4096]{2,1,0:T(4,128)} %bitcast.9), custom_call_target="tpu_custom_call" | custom-call | tf_op jit(solution)/shard_map/krylov_qr/pallas_call | solution.py:393
  84.4 0.7 copy.7
  85.1 0.6 copy.8
Async XLA Ops:
  0.6 0.8 copy-start

commit v4 on v3

--- a/solution.py
+++ b/solution.py
@@ -14,6 +14,8 @@
 ELEMS = 8
 LANES = 128
 PANEL = 16
+LEAD = 3
+LATE = POWERS + 1 - LEAD
 F32 = jnp.float32
 BF16 = jnp.bfloat16
 PAIRS = ((0, 5), (6, None), (1, 2), (3, 4))
@@ -94,46 +96,68 @@
     return out
 
 
+def forward(column, below, later, r, corner, start):
+    at = lane((PANEL, LANES))
+    for j in range(PANEL):
+        inv = lax.rsqrt(pick(column[j], j))
+        r[j] = r[j] * inv
+        scaled = column[j] * inv
+        corner = jnp.where(at == start + j, scaled, corner)
+        for m in range(j + 1, PANEL):
+            s = pick(scaled, m)
+            column[m] = column[m] - scaled * s
+            r[m] = r[m] - s * r[j]
+        if below is not None:
+            below[j] = below[j] * inv
+            for m in range(j + 1, PANEL):
+                below[m] = below[m] - below[j] * pick(scaled, m)
+            later = later - below[j] * r[j]
+    return later, jnp.where(at <= row((PANEL, LANES)) + start, corner, 0.0)
+
+
 def eliminate(full):
     later = full
+    count = full.shape[0]
     upper, diagonal, inverse = [], [], []
-    for p in range(COLS // PANEL):
-        start = PANEL * p
-        more = p < COLS // PANEL - 1
+    at = lane((PANEL, LANES))
+    for start in range(0, count, PANEL):
+        more = start + PANEL < count
         column = [spread(later[:PANEL], start + j) for j in range(PANEL)]
         below = [spread(later[PANEL:], start + j) for j in range(PANEL)] if more else None
-        at = lane(later.shape)
-        own = (at >= start) & (at < start + PANEL)
-        later = jnp.where(own, (row(later.shape) + start == at).astype(F32), later)
+        lanes = lane(later.shape)
+        own = (lanes >= start) & (lanes < start + PANEL)
+        later = jnp.where(own, (row(later.shape) + start == lanes).astype(F32), later)
         first, later = later[:PANEL], later[PANEL:]
         r = [pick(first, j) for j in range(PANEL)]
-        at = lane((PANEL, LANES))
-        corner = jnp.zeros((PANEL, LANES), F32)
-        for j in range(PANEL):
-            inv = lax.rsqrt(pick(column[j], j))
-            r[j] = r[j] * inv
-            scaled = column[j] * inv
-            corner = jnp.where(at == start + j, scaled, corner)
-            for m in range(j + 1, PANEL):
-                s = pick(scaled, m)
-                column[m] = column[m] - scaled * s
-                r[m] = r[m] - s * r[j]
-            if more:
-                below[j] = below[j] * inv
-                for m in range(j + 1, PANEL):
-                    below[m] = below[m] - below[j] * pick(scaled, m)
-                later = later - below[j] * r[j]
+        later, corner = forward(column, below, later, r, jnp.zeros((PANEL, LANES), F32), start)
         rows = stacked(r)
         inverse.append(jnp.where(at < start + PANEL, rows, 0.0))
         upper.append(jnp.where(at >= start + PANEL, rows, 0.0))
-        diagonal.append(jnp.where(at <= row((PANEL, LANES)) + start, corner, 0.0))
-    below = jnp.concatenate(diagonal + [jnp.zeros((LANES - COLS, LANES), F32)], axis=0)
-    return jnp.concatenate(upper, axis=0) + below.T[:COLS], jnp.concatenate(inverse, axis=0)
+        diagonal.append(corner)
+    below = jnp.concatenate(diagonal + [jnp.zeros((LANES - count, LANES), F32)], axis=0)
+    return jnp.concatenate(upper, axis=0) + below.T[:count], jnp.concatenate(inverse, axis=0)
+
+
+def eliminate_row(a, w, w_t, k):
+    start = PANEL * k
+    at = lane((PANEL, LANES))
+    own = (at >= start) & (at < start + PANEL)
+    lead = dot_exact(a, w_t)
+    placed = jnp.concatenate(
+        [jnp.zeros((start, LANES), F32), lead, jnp.zeros((LANES - start - PANEL, LANES), F32)], axis=0
+    )
+    rest = a - dot_exact(lead, placed.T)
+    first = jnp.where(own, (row((PANEL, LANES)) + start == at).astype(F32), -dot_exact(lead, w))
+    column = [spread(rest, start + j) for j in range(PANEL)]
+    r = [pick(first, j) for j in range(PANEL)]
+    _, corner = forward(column, None, None, r, jnp.zeros((PANEL, LANES), F32), start)
+    return lead + corner, jnp.where(at < start + PANEL, stacked(r), 0.0)
 
 
 def kernel(sizes, rhs_ref, blocks_ref, basis_ref, factor_ref, raw, b_f32, b_parts, vecs, ypack, hx, hy,
-           u_ref, packed, stage_a, stage_b, stage_c, sum_a, sum_b, sum_c, gathered, r_ref,
-           load_sem, hsend, hrecv, asend, arecv, word):
+           u_ref, packed, stage_a, stage_b, stage_c, sum_a, sum_b, sum_c, gathered,
+           halves, other_half, late_sum, late_yx, late_z, late_both,
+           load_sem, hsend, hrecv, asend, arecv, lsend, lrecv, word):
     ny, nz, nc, nx = sizes
     gx, gy = ny * nz * nc, nx
     me_x, me_y = lax.axis_index("gx"), lax.axis_index("gy")
@@ -154,6 +178,8 @@
 
     def mate_z(i):
         return place(at_y, i, core, me_y)
+
+    me_yx, n_yx = at_y * nx + me_y, ny * nx
 
     groups = ((n_g, me_g, mate_g), (ny, at_y, mate_y), (nz, at_z, mate_z))
     near = (
@@ -173,8 +199,10 @@
     def at_distance(d):
         peers = []
         for n, me, mate in groups[1:]:
-            if d == 1 or 2 * d <= n // 2:
-                peers += [mate(lax.rem(me + d, n)), mate(lax.rem(me + n - d, n))]
+            if 2 * d <= n:
+                peers.append(mate(lax.rem(me + d, n)))
+            if 2 * d < n:
+                peers.append(mate(lax.rem(me + n - d, n)))
         return peers
 
     greeted = list(near) + at_distance(1)
@@ -260,9 +288,140 @@
             out = jnp.where(lanes // 16 == e, total[DOF * e : DOF * (e + 1)], out)
         return out
 
-    known = [at_distance(d) for d in (1, 2, 4) if 2 * d <= max(ny, nz) // 2]
+    known = [at_distance(d) for d in (1, 2, 4)]
     at_cell = (lanes // 16) % 4
     zero = jnp.zeros((DOF, LANES), F32)
+    def all_bytes(buffer, n, sem):
+        return pltpu.make_async_copy(buffer.at[pl.ds(0, n - 1)], buffer.at[pl.ds(0, n - 1)], sem)
+
+    def add_up(buffer, n):
+        parts = [buffer[i] for i in range(n)]
+        while len(parts) > 1:
+            parts = [parts[i] + parts[i + 1] for i in range(0, len(parts), 2)]
+        return parts[0]
+
+    def far_first(i, n):
+        return lax.rem(n // 2 + (1 - 2 * lax.rem(i, 2)) * lax.div(i, 2), n)
+
+    piece = 2 * RHS // n_g
+
+    def send_pieces(n, me, mate, src, dst, sem):
+        number, stage = sem
+
+        @pl.loop(1, n)
+        def _(i):
+            other = lax.rem(me + far_first(i, n), n)
+            remote(src(other), dst, asend.at[number, stage], arecv.at[number, stage], mate(other)).start()
+
+    def lead_0(number, gram):
+        low = lane((2 * RHS, LANES)) < 64
+        both = jnp.where(low, gram[: 2 * RHS], pltpu.roll(gram[2 * RHS : 4 * RHS], 64, 1))
+        for i in range(n_g):
+            packed[number, i] = both[piece * i : piece * (i + 1)]
+        send_pieces(n_g, me_g, mate_g, lambda i: packed.at[number, i], stage_a.at[number, me_g], (number, 0))
+        stage_a[number, me_g] = packed[number, me_g]
+
+    def lead_1(number):
+        all_bytes(stage_a.at[number], n_g, arecv.at[number, 0]).wait()
+        sum_a[number] = add_up(stage_a.at[number], n_g)
+        send_pieces(ny, at_y, mate_y, lambda i: sum_a.at[number], stage_b.at[number, at_y], (number, 1))
+        stage_b[number, at_y] = sum_a[number]
+
+    def lead_2(number):
+        all_bytes(stage_b.at[number], ny, arecv.at[number, 1]).wait()
+        sum_b[number] = add_up(stage_b.at[number], ny)
+        send_pieces(nz, at_z, mate_z, lambda i: sum_b.at[number], stage_c.at[number, at_z], (number, 2))
+        stage_c[number, at_z] = sum_b[number]
+
+    def lead_3(number):
+        all_bytes(stage_c.at[number], nz, arecv.at[number, 2]).wait()
+        sum_c[number] = add_up(stage_c.at[number], nz)
+        send_pieces(n_g, me_g, mate_g, lambda i: sum_c.at[number], gathered.at[number, me_g], (number, 3))
+        gathered[number, me_g] = sum_c[number]
+
+    def lead_4(number):
+        all_bytes(gathered.at[number], n_g, arecv.at[number, 3]).wait()
+        both = jnp.concatenate([gathered[number, i] for i in range(n_g)], axis=0)
+        full = jnp.concatenate([both, pltpu.roll(both, 64, 1)], axis=0)[: LEAD * RHS]
+        return jnp.where(lane(full.shape) < LEAD * RHS, full, 0.0)
+
+    partner = place(at_y, at_z, nc - 1 - core, me_y)
+
+    def to_partner(number, c, stage):
+        if stage == 0:
+            src, dst = halves.at[number, c, nc - 1 - core], other_half.at[number, c]
+        else:
+            src, dst = late_sum.at[number, c, 2], late_both.at[number, c, core]
+        return remote(src, dst, lsend.at[number, c, stage], lrecv.at[number, c, stage], partner)
+
+    def late_0(number, k, rows):
+        c = k - LEAD
+        halves[number, c, 0] = rows[:8]
+        halves[number, c, 1] = rows[8:]
+        to_partner(number, c, 0).start()
+
+    def late_1(number, k):
+        c = k - LEAD
+        to_partner(number, c, 0).wait_recv()
+        total = halves[number, c, core] + other_half[number, c]
+        late_sum[number, c, 0] = total
+
+        @pl.loop(0, n_yx - 1)
+        def _(j):
+            y = lax.rem(at_y + far_first(lax.div(j, nx) + 1, ny), ny)
+            x = lax.rem(me_y + lax.rem(j, nx) + 1, nx)
+            remote(
+                late_sum.at[number, c, 0], late_yx.at[number, c, me_yx],
+                lsend.at[number, c, 1], lrecv.at[number, c, 1], place(y, at_z, core, x),
+            ).start()
+
+        late_yx[number, c, me_yx] = total
+
+    def late_2(number, k):
+        c = k - LEAD
+        all_bytes(late_yx.at[number, c], n_yx, lrecv.at[number, c, 1]).wait()
+        total = add_up(late_yx.at[number, c], n_yx)
+        late_sum[number, c, 1] = total
+
+        @pl.loop(1, nz)
+        def _(i):
+            other = lax.rem(at_z + far_first(i, nz), nz)
+            remote(
+                late_sum.at[number, c, 1], late_z.at[number, c, at_z],
+                lsend.at[number, c, 2], lrecv.at[number, c, 2], mate_z(other),
+            ).start()
+
+        late_z[number, c, at_z] = total
+
+    def late_3(number, k):
+        c = k - LEAD
+        all_bytes(late_z.at[number, c], nz, lrecv.at[number, c, 2]).wait()
+        total = add_up(late_z.at[number, c], nz)
+        late_sum[number, c, 2] = total
+        to_partner(number, c, 3).start()
+        late_both[number, c, core] = total
+
+    def late_4(number, k):
+        c = k - LEAD
+        to_partner(number, c, 3).wait_recv()
+        return jnp.concatenate([late_both[number, c, 0], late_both[number, c, 1]], axis=0)
+
+    def gram_of(number):
+        u = u_ref[number]
+        return dot_exact(u, u, 0)
+
+    def gram_rows(number, k):
+        return gram_of(number)[RHS * k : RHS * (k + 1)]
+
+    u_lane = lane((ELEMS * DOF, LANES)) // RHS
+
+    def add_column(k, v):
+        for e in range(ELEMS):
+            here = slice(DOF * e, DOF * (e + 1))
+            shift = (RHS * (k - e)) % LANES
+            turned = pltpu.roll(v, shift, 1) if shift else v
+            u_ref[0, here] = jnp.where(lanes // RHS == k, turned, u_ref[0, here])
+
     for k in range(POWERS):
         z_low = jnp.where(at_cell == 0, 0.0, pltpu.roll(v, 16, 1))
         z_high = jnp.where(at_cell == 3, 0.0, pltpu.roll(v, LANES - 16, 1))
@@ -271,6 +430,16 @@
         if k < len(known):
             for peer in known[k]:
                 signal(word.at[k], peer)
+        if k == LEAD - 1:
+            columns = transpose_arrays([vecs[i] for i in range(LEAD)] + [zero] * (8 - LEAD))
+            for e in range(ELEMS):
+                u_ref[0, DOF * e : DOF * (e + 1), :] = columns[e]
+            lead_0(0, gram_of(0))
+        if k == LEAD:
+            add_column(k, v)
+            late_0(0, k, gram_rows(0, k))
+            lead_1(0)
+            late_1(0, k)
         for copy in sends[k]:
             copy.wait_recv()
         x_low = jnp.where(me_x > 0, hx[k, 0], 0.0)
@@ -285,94 +454,105 @@
             [jnp.where(half, own_low, pltpu.roll(y_high, 64, 1)), jnp.where(half, own_high, y_high)], axis=0
         )
         outer = product(1, [x_low, x_high, y_low, y_high])
-        if k < len(known):
-            pl.semaphore_wait(word.at[k], len(known[k]))
         v = inner + outer
         if k < POWERS - 1:
             sends.append(publish(k + 1, v))
-        else:
-            vecs[POWERS] = v
-
-    columns = transpose_arrays([vecs[k] for k in range(POWERS + 1)] + [zero] * (7 - POWERS))
-    for e in range(ELEMS):
-        u_ref[DOF * e : DOF * (e + 1), :] = columns[e]
-
-    def all_bytes(buffer, n, sem):
-        return pltpu.make_async_copy(buffer.at[pl.ds(0, n - 1)], buffer.at[pl.ds(0, n - 1)], sem)
-
-    def add_up(buffer, n):
-        total = buffer[0]
-        for i in range(1, n):
-            total = total + buffer[i]
-        return total
-
-    def one_pass(number, _):
-        u = u_ref[...]
-        gram = dot_exact(u, u, 0)[:COLS]
-        def block(k, to):
-            part = gram[RHS * k : RHS * (k + 1)]
-            return pltpu.roll(part, (to - RHS * k) % LANES, 1) if (to - RHS * k) % LANES else part
-
-        lane16 = lane((RHS, LANES))
-        top = jnp.where(lane16 < 80, block(0, 0), block(2, 80))
-        low = jnp.where(lane16 < 64, block(1, 0), jnp.where(lane16 < 96, block(3, 64), block(4, 96)))
-        both = jnp.concatenate([top, low], axis=0)
-        piece = 2 * RHS // n_g
-        for i in range(n_g):
-            packed[number, i] = both[piece * i : piece * (i + 1)]
-
-        def start_all(n, me, mate, src, dst, sem):
-            for d in sorted(range(1, n), key=lambda d: -min(d, n - d)):
-                other = lax.rem(me + d, n)
-                remote(src(other), dst, asend.at[number, sem], arecv.at[number, sem], mate(other)).start()
-
-        start_all(n_g, me_g, mate_g, lambda i: packed.at[number, i], stage_a.at[number, me_g], 0)
-        stage_a[number, me_g] = packed[number, me_g]
-        all_bytes(stage_a.at[number], n_g, arecv.at[number, 0]).wait()
-        sum_a[number] = add_up(stage_a.at[number], n_g)
-        start_all(ny, at_y, mate_y, lambda i: sum_a.at[number], stage_b.at[number, at_y], 1)
-        stage_b[number, at_y] = sum_a[number]
-        all_bytes(stage_b.at[number], ny, arecv.at[number, 1]).wait()
-        sum_b[number] = add_up(stage_b.at[number], ny)
-        start_all(nz, at_z, mate_z, lambda i: sum_b.at[number], stage_c.at[number, at_z], 2)
-        stage_c[number, at_z] = sum_b[number]
-        all_bytes(stage_c.at[number], nz, arecv.at[number, 2]).wait()
-        sum_c[number] = add_up(stage_c.at[number], nz)
-        start_all(n_g, me_g, mate_g, lambda i: sum_c.at[number], gathered.at[number, me_g], 3)
-        gathered[number, me_g] = sum_c[number]
-        all_bytes(gathered.at[number], n_g, arecv.at[number, 3]).wait()
-
-        both = jnp.concatenate([gathered[number, i] for i in range(n_g)], axis=0)
-        top, low = both[:RHS], both[RHS:]
-        blocks_of = (
-            (top, 0, 80), (low, 0, 64), (top, 80, 48), (low, 64, 32), (low, 96, 16)
-        )
-        upper = []
-        for k, (source, at, width) in enumerate(blocks_of):
-            shift = (RHS * k - at) % LANES
-            part = pltpu.roll(source, shift, 1) if shift else source
-            upper.append(jnp.where((lane16 >= RHS * k) & (lane16 < COLS), part, 0.0))
-        upper = jnp.concatenate(upper + [jnp.zeros((LANES - COLS, LANES), F32)], axis=0)
-        r_, c_ = row((LANES, LANES)), lane((LANES, LANES))
-        full = jnp.where(r_ // RHS <= c_ // RHS, upper, upper.T)
-        factor, inverse = eliminate(full[:COLS])
-        r_ref[number] = factor
-        inverse = jnp.concatenate([inverse, jnp.zeros((LANES - COLS, LANES), F32)], axis=0)
-        u_ref[...] = dot_exact(u, inverse.T)
-        return 0
-
-    lax.fori_loop(0, 2, one_pass, 0)
-
-    pad = jnp.zeros((LANES - COLS, LANES), F32)
-    factor = dot_exact(r_ref[1], jnp.concatenate([r_ref[0], pad], axis=0))
-    factor_ref[...] = factor[:, :COLS]
-    columns = transpose_arrays([u_ref[DOF * e : DOF * (e + 1), :] for e in range(ELEMS)])
-    for k in range(POWERS + 1):
-        out = transpose_groups(columns[k])
+        if k < len(known):
+            pl.semaphore_wait(word.at[k], len(known[k]))
+
+    def padded(rows, start=0):
+        parts = [rows, jnp.zeros((LANES - start - rows.shape[0], LANES), F32)]
+        if start:
+            parts.insert(0, jnp.zeros((start, LANES), F32))
+        return jnp.concatenate(parts, axis=0)
+
+    class Pass:
+        pass
+
+    passes = [Pass(), Pass()]
+
+    def solve_lead(number):
+        p = passes[number]
+        p.r, w = eliminate(lead_4(number))
+        p.w = padded(w)
+        p.w_t = p.w.T
+        p.l = None
+
+    def apply_lead(number):
+        return dot_exact(u_ref[number], passes[number].w_t)
+
+    def solve_late(number, k):
+        p = passes[number]
+        l_k, w_k = eliminate_row(late_4(number, k), p.w, p.w_t, k)
+        l_k = padded(l_k, RHS * k)
+        p.l = l_k if p.l is None else p.l + l_k
+        if k < POWERS:
+            p.w = p.w + padded(w_k, RHS * k)
+            p.w_t = p.w.T
+        return dot_exact(u_ref[number], jnp.concatenate([w_k] * (LANES // RHS), axis=0).T)
+
+    def next_lead():
+        u_ref[1] = apply_lead(0)
+        lead_0(1, gram_of(1))
+
+    def next_late(k):
+        q = solve_late(0, k)
+        u_ref[1] = jnp.where(u_lane == k, q, u_ref[1])
+        late_0(1, k, gram_rows(1, k))
+
+    def factor_of(number):
+        p = passes[number]
+        return padded(p.r) + p.l.T
+
+    def give(k, column):
+        out = transpose_groups(column)
         for t in range(8):
             at = slice(LANES * t, LANES * (t + 1))
             basis_ref[k, 0, :, at] = out[8 * t : 8 * t + 4]
             basis_ref[k, 1, :, at] = out[8 * t + 4 : 8 * t + 8]
+
+    def give_lead():
+        q = apply_lead(1)
+        columns = transpose_arrays([q[DOF * e : DOF * (e + 1), :] for e in range(ELEMS)])
+        for k in range(LEAD):
+            give(k, columns[k])
+
+    def give_late(k):
+        q = solve_late(1, k)
+        column = q[:DOF]
+        for e in range(1, ELEMS):
+            column = jnp.where(lanes // RHS == e, q[DOF * e : DOF * (e + 1)], column)
+        give(k, column)
+
+    last, before = POWERS, POWERS - 1
+    add_column(last, v)
+    late_0(0, last, gram_rows(0, last))
+    lead_2(0)
+    late_1(0, last)
+    late_2(0, before)
+    lead_3(0)
+    late_2(0, last)
+    late_3(0, before)
+    solve_lead(0)
+    next_lead()
+    next_late(before)
+    late_3(0, last)
+    late_1(1, before)
+    lead_1(1)
+    next_late(last)
+    first_r = factor_of(0)
+    late_1(1, last)
+    lead_2(1)
+    late_2(1, before)
+    late_2(1, last)
+    lead_3(1)
+    late_3(1, before)
+    solve_lead(1)
+    late_3(1, last)
+    give_late(before)
+    give_late(last)
+    factor_ref[...] = dot_exact(factor_of(1)[:COLS], first_r)[:, :COLS]
+    give_lead()
 
     for copies in sends:
         for copy in copies:
@@ -382,6 +562,11 @@
         all_bytes(stage_b.at[number], ny, asend.at[number, 1]).wait()
         all_bytes(stage_c.at[number], nz, asend.at[number, 2]).wait()
         all_bytes(gathered.at[number], n_g, asend.at[number, 3]).wait()
+        for c in range(LATE):
+            to_partner(number, c, 0).wait_send()
+            all_bytes(late_yx.at[number, c], n_yx, lsend.at[number, c, 1]).wait()
+            all_bytes(late_z.at[number, c], nz, lsend.at[number, c, 2]).wait()
+            to_partner(number, c, 3).wait_send()
 
 
 def on_device(sizes, rhs, blocks):
@@ -406,7 +591,7 @@
             vmem((POWERS, 2, DOF // 2, LANES), F32),
             vmem((POWERS, 2, DOF, LANES), F32),
             vmem((POWERS, 2, DOF // 2, LANES), F32),
-            vmem((ELEMS * DOF, LANES), F32),
+            vmem((2, ELEMS * DOF, LANES), F32),
             vmem((2, n_g, piece, LANES), F32),
             vmem((2, n_g, piece, LANES), F32),
             vmem((2, ny, piece, LANES), F32),
@@ -415,12 +600,19 @@
             vmem((2, piece, LANES), F32),
             vmem((2, piece, LANES), F32),
             vmem((2, n_g, piece, LANES), F32),
-            vmem((2, COLS, LANES), F32),
+            vmem((2, LATE, 2, 8, LANES), F32),
+            vmem((2, LATE, 8, LANES), F32),
+            vmem((2, LATE, 3, 8, LANES), F32),
+            vmem((2, LATE, ny * nx, 8, LANES), F32),
+            vmem((2, LATE, nz, 8, LANES), F32),
+            vmem((2, LATE, 2, 8, LANES), F32),
             pltpu.SemaphoreType.DMA((1,)),
             pltpu.SemaphoreType.DMA((POWERS, 4)),
             pltpu.SemaphoreType.DMA((POWERS, 4)),
             pltpu.SemaphoreType.DMA((2, 4)),
             pltpu.SemaphoreType.DMA((2, 4)),
+            pltpu.SemaphoreType.DMA((2, LATE, 4)),
+            pltpu.SemaphoreType.DMA((2, LATE, 4)),
             pltpu.SemaphoreType.REGULAR((POWERS,)),
         ],
         compiler_params=pltpu.CompilerParams(

time: 85.9 us -> 80.7 us (0.939)
  Pallas kernels: 83 us -> 77.8 us
    pallas_call x1, Pallas kernels: 83 us -> 77.8 us  [on_device(): pl.pallas_call(functools.partial(kernel, sizes), out_shape=(jax.ShapeDtyp...]
where the time goes in v4:
time: 80.7 us; the launch traced here: 80.5 us
  Pallas kernels  77.8 us (96%)
  local copies, waits for them, and re-layouts  2.04 us (3%)
    pallas_call x1, Pallas kernels, on_device(): pl.pallas_call(functools.partial(kernel, sizes), out_shape=(jax.ShapeDtyp...  77.8 us
    unnamed x4, local copies, waits for them, and re-layouts  2.04 us

profile of v4, /device:TPU:1, one launch (start us, length us, event | category | flops | bytes accessed | tf_op | source)
XLA Modules:
  0.0 80.5 jit_solution(1702155234865240178)
XLA Ops:
  0.6 0.0 copy-start
  0.6 0.7 copy-done
  1.4 77.8 %krylov_qr.1 = (f32[5,2,4,1024]{3,2,1,0:T(4,128)S(1)}, f32[80,80]{1,0:T(8,128)S(1)}) custom-call(f32[2,4,1024]{2,1,0:T(4,128)S(1)} %bitcast.8, f32[14,4,4096]{2,1,0:T(4,128)} %bitcast.9), custom_call_target="tpu_custom_call" | custom-call | tf_op jit(solution)/shard_map/krylov_qr/pallas_call | solution.py:578
  79.2 0.7 copy.7
  79.9 0.6 copy.8
Async XLA Ops:
  0.6 0.8 copy-start

commit v5 on v4

--- a/solution.py
+++ b/solution.py
@@ -15,7 +15,7 @@
 LANES = 128
 PANEL = 16
 LEAD = 3
-LATE = POWERS + 1 - LEAD
+CHUNKS = POWERS + 2 - LEAD
 F32 = jnp.float32
 BF16 = jnp.bfloat16
 PAIRS = ((0, 5), (6, None), (1, 2), (3, 4))
@@ -155,9 +155,8 @@
 
 
 def kernel(sizes, rhs_ref, blocks_ref, basis_ref, factor_ref, raw, b_f32, b_parts, vecs, ypack, hx, hy,
-           u_ref, packed, stage_a, stage_b, stage_c, sum_a, sum_b, sum_c, gathered,
-           halves, other_half, late_sum, late_yx, late_z, late_both,
-           load_sem, hsend, hrecv, asend, arecv, lsend, lrecv, word):
+           u_ref, halves, other_half, sums, from_yx, from_z, whole,
+           load_sem, hsend, hrecv, csend, crecv, word):
     ny, nz, nc, nx = sizes
     gx, gy = ny * nz * nc, nx
     me_x, me_y = lax.axis_index("gx"), lax.axis_index("gy")
@@ -167,12 +166,6 @@
     def place(y, z, c, x):
         return {"gx": (y * nz + z) * nc + c, "gy": x}
 
-    me_g = me_y * nc + core
-    n_g = nx * nc
-
-    def mate_g(i):
-        return place(at_y, at_z, lax.rem(i, nc), lax.div(i, nc))
-
     def mate_y(i):
         return place(i, at_z, core, me_y)
 
@@ -180,8 +173,7 @@
         return place(at_y, i, core, me_y)
 
     me_yx, n_yx = at_y * nx + me_y, ny * nx
-
-    groups = ((n_g, me_g, mate_g), (ny, at_y, mate_y), (nz, at_z, mate_z))
+    lines = ((ny, at_y, mate_y), (nz, at_z, mate_z))
     near = (
         {"gx": lax.rem(me_x + gx - 1, gx), "gy": me_y},
         {"gx": lax.rem(me_x + 1, gx), "gy": me_y},
@@ -198,19 +190,18 @@
 
     def at_distance(d):
         peers = []
-        for n, me, mate in groups[1:]:
+        for n, me, mate in lines:
             if 2 * d <= n:
                 peers.append(mate(lax.rem(me + d, n)))
             if 2 * d < n:
                 peers.append(mate(lax.rem(me + n - d, n)))
         return peers
 
-    greeted = list(near) + at_distance(1)
+    known = [at_distance(d) for d in (1, 2, 4)]
+    greeted = list(near) + known[0] + [{"gx": me_x, "gy": lax.rem(me_y + d, nx)} for d in range(2, nx - 1)]
     for peer in greeted:
         signal(barrier, peer)
-    for d in range(1, n_g):
-        signal(barrier, mate_g(lax.rem(me_g + d, n_g)))
-    count = len(greeted) + n_g - 1
+    count = len(greeted)
 
     flat_rhs = jnp.concatenate([rhs_ref[0], rhs_ref[1]], axis=0)
     first = jnp.concatenate([flat_rhs[:, LANES * t : LANES * (t + 1)] for t in range(8)], axis=0)
@@ -273,6 +264,15 @@
     v = transpose_groups(first)
     pl.semaphore_wait(barrier, count)
     sends = [publish(0, v)]
+
+    def tell(step):
+        for peer in known[step]:
+            signal(word.at[step], peer)
+
+    def hear(step):
+        pl.semaphore_wait(word.at[step], len(known[step]))
+
+    tell(0)
     load.wait()
     prepare((0, 1))
     prepare((2, 3))
@@ -288,9 +288,14 @@
             out = jnp.where(lanes // 16 == e, total[DOF * e : DOF * (e + 1)], out)
         return out
 
-    known = [at_distance(d) for d in (1, 2, 4)]
     at_cell = (lanes // 16) % 4
     zero = jnp.zeros((DOF, LANES), F32)
+    def padded(rows, start=0):
+        parts = [rows, jnp.zeros((LANES - start - rows.shape[0], LANES), F32)]
+        if start:
+            parts.insert(0, jnp.zeros((start, LANES), F32))
+        return jnp.concatenate(parts, axis=0)
+
     def all_bytes(buffer, n, sem):
         return pltpu.make_async_copy(buffer.at[pl.ds(0, n - 1)], buffer.at[pl.ds(0, n - 1)], sem)
 
@@ -303,115 +308,85 @@
     def far_first(i, n):
         return lax.rem(n // 2 + (1 - 2 * lax.rem(i, 2)) * lax.div(i, 2), n)
 
-    piece = 2 * RHS // n_g
-
-    def send_pieces(n, me, mate, src, dst, sem):
-        number, stage = sem
-
-        @pl.loop(1, n)
-        def _(i):
-            other = lax.rem(me + far_first(i, n), n)
-            remote(src(other), dst, asend.at[number, stage], arecv.at[number, stage], mate(other)).start()
-
-    def lead_0(number, gram):
-        low = lane((2 * RHS, LANES)) < 64
-        both = jnp.where(low, gram[: 2 * RHS], pltpu.roll(gram[2 * RHS : 4 * RHS], 64, 1))
-        for i in range(n_g):
-            packed[number, i] = both[piece * i : piece * (i + 1)]
-        send_pieces(n_g, me_g, mate_g, lambda i: packed.at[number, i], stage_a.at[number, me_g], (number, 0))
-        stage_a[number, me_g] = packed[number, me_g]
-
-    def lead_1(number):
-        all_bytes(stage_a.at[number], n_g, arecv.at[number, 0]).wait()
-        sum_a[number] = add_up(stage_a.at[number], n_g)
-        send_pieces(ny, at_y, mate_y, lambda i: sum_a.at[number], stage_b.at[number, at_y], (number, 1))
-        stage_b[number, at_y] = sum_a[number]
-
-    def lead_2(number):
-        all_bytes(stage_b.at[number], ny, arecv.at[number, 1]).wait()
-        sum_b[number] = add_up(stage_b.at[number], ny)
-        send_pieces(nz, at_z, mate_z, lambda i: sum_b.at[number], stage_c.at[number, at_z], (number, 2))
-        stage_c[number, at_z] = sum_b[number]
-
-    def lead_3(number):
-        all_bytes(stage_c.at[number], nz, arecv.at[number, 2]).wait()
-        sum_c[number] = add_up(stage_c.at[number], nz)
-        send_pieces(n_g, me_g, mate_g, lambda i: sum_c.at[number], gathered.at[number, me_g], (number, 3))
-        gathered[number, me_g] = sum_c[number]
-
-    def lead_4(number):
-        all_bytes(gathered.at[number], n_g, arecv.at[number, 3]).wait()
-        both = jnp.concatenate([gathered[number, i] for i in range(n_g)], axis=0)
-        full = jnp.concatenate([both, pltpu.roll(both, 64, 1)], axis=0)[: LEAD * RHS]
-        return jnp.where(lane(full.shape) < LEAD * RHS, full, 0.0)
-
     partner = place(at_y, at_z, nc - 1 - core, me_y)
 
     def to_partner(number, c, stage):
         if stage == 0:
             src, dst = halves.at[number, c, nc - 1 - core], other_half.at[number, c]
         else:
-            src, dst = late_sum.at[number, c, 2], late_both.at[number, c, core]
-        return remote(src, dst, lsend.at[number, c, stage], lrecv.at[number, c, stage], partner)
-
-    def late_0(number, k, rows):
-        c = k - LEAD
+            src, dst = sums.at[number, c, 2], whole.at[number, c, core]
+        return remote(src, dst, csend.at[number, c, stage], crecv.at[number, c, stage], partner)
+
+    def start_sum(number, c, rows):
         halves[number, c, 0] = rows[:8]
         halves[number, c, 1] = rows[8:]
         to_partner(number, c, 0).start()
 
-    def late_1(number, k):
-        c = k - LEAD
+    def over_yx(number, c):
         to_partner(number, c, 0).wait_recv()
         total = halves[number, c, core] + other_half[number, c]
-        late_sum[number, c, 0] = total
+        sums[number, c, 0] = total
 
         @pl.loop(0, n_yx - 1)
         def _(j):
             y = lax.rem(at_y + far_first(lax.div(j, nx) + 1, ny), ny)
             x = lax.rem(me_y + lax.rem(j, nx) + 1, nx)
             remote(
-                late_sum.at[number, c, 0], late_yx.at[number, c, me_yx],
-                lsend.at[number, c, 1], lrecv.at[number, c, 1], place(y, at_z, core, x),
+                sums.at[number, c, 0], from_yx.at[number, c, me_yx],
+                csend.at[number, c, 1], crecv.at[number, c, 1], place(y, at_z, core, x),
             ).start()
 
-        late_yx[number, c, me_yx] = total
-
-    def late_2(number, k):
-        c = k - LEAD
-        all_bytes(late_yx.at[number, c], n_yx, lrecv.at[number, c, 1]).wait()
-        total = add_up(late_yx.at[number, c], n_yx)
-        late_sum[number, c, 1] = total
+        from_yx[number, c, me_yx] = total
+
+    def over_z(number, c):
+        all_bytes(from_yx.at[number, c], n_yx, crecv.at[number, c, 1]).wait()
+        total = add_up(from_yx.at[number, c], n_yx)
+        sums[number, c, 1] = total
 
         @pl.loop(1, nz)
         def _(i):
             other = lax.rem(at_z + far_first(i, nz), nz)
             remote(
-                late_sum.at[number, c, 1], late_z.at[number, c, at_z],
-                lsend.at[number, c, 2], lrecv.at[number, c, 2], mate_z(other),
+                sums.at[number, c, 1], from_z.at[number, c, at_z],
+                csend.at[number, c, 2], crecv.at[number, c, 2], mate_z(other),
             ).start()
 
-        late_z[number, c, at_z] = total
-
-    def late_3(number, k):
-        c = k - LEAD
-        all_bytes(late_z.at[number, c], nz, lrecv.at[number, c, 2]).wait()
-        total = add_up(late_z.at[number, c], nz)
-        late_sum[number, c, 2] = total
+        from_z[number, c, at_z] = total
+
+    def share(number, c):
+        all_bytes(from_z.at[number, c], nz, crecv.at[number, c, 2]).wait()
+        total = add_up(from_z.at[number, c], nz)
+        sums[number, c, 2] = total
         to_partner(number, c, 3).start()
-        late_both[number, c, core] = total
-
-    def late_4(number, k):
-        c = k - LEAD
+        whole[number, c, core] = total
+
+    def finish_sum(number, c):
         to_partner(number, c, 3).wait_recv()
-        return jnp.concatenate([late_both[number, c, 0], late_both[number, c, 1]], axis=0)
+        return jnp.concatenate([whole[number, c, 0], whole[number, c, 1]], axis=0)
 
     def gram_of(number):
         u = u_ref[number]
         return dot_exact(u, u, 0)
 
-    def gram_rows(number, k):
-        return gram_of(number)[RHS * k : RHS * (k + 1)]
+    lane16 = lane((RHS, LANES))
+
+    def start_lead(number):
+        gram = gram_of(number)
+        one, two, three = gram[:RHS], gram[RHS : 2 * RHS], gram[2 * RHS : 3 * RHS]
+        one, two = pltpu.roll(one, 5 * RHS, 1), pltpu.roll(two, 3 * RHS, 1)
+        start_sum(number, 0, jnp.where(lane16 < 3 * RHS, three, jnp.where(lane16 < 5 * RHS, two, one)))
+
+    def finish_lead(number):
+        rows = finish_sum(number, 0)
+        one = jnp.where(lane16 < RHS, pltpu.roll(rows, 3 * RHS, 1), 0.0)
+        two = jnp.where(lane16 < 2 * RHS, pltpu.roll(rows, 5 * RHS, 1), 0.0)
+        three = jnp.where(lane16 < 3 * RHS, rows, 0.0)
+        lower = padded(jnp.concatenate([one, two, three], axis=0))
+        at = row((LANES, LANES)) // RHS >= lane((LANES, LANES)) // RHS
+        return jnp.where(at, lower, lower.T)[: LEAD * RHS]
+
+    def start_row(number, k):
+        start_sum(number, k - LEAD + 1, gram_of(number)[RHS * k : RHS * (k + 1)])
 
     u_lane = lane((ELEMS * DOF, LANES)) // RHS
 
@@ -427,19 +402,19 @@
         z_high = jnp.where(at_cell == 3, 0.0, pltpu.roll(v, LANES - 16, 1))
         inner = v + product(0, [v, z_low, z_high, zero])
         swapped = pltpu.roll(v, 64, 1)
-        if k < len(known):
-            for peer in known[k]:
-                signal(word.at[k], peer)
+        if k < len(known) - 1:
+            hear(k)
+            tell(k + 1)
         if k == LEAD - 1:
             columns = transpose_arrays([vecs[i] for i in range(LEAD)] + [zero] * (8 - LEAD))
             for e in range(ELEMS):
                 u_ref[0, DOF * e : DOF * (e + 1), :] = columns[e]
-            lead_0(0, gram_of(0))
+            start_lead(0)
+            over_yx(0, 0)
         if k == LEAD:
             add_column(k, v)
-            late_0(0, k, gram_rows(0, k))
-            lead_1(0)
-            late_1(0, k)
+            start_row(0, k)
+            over_yx(0, 1)
         for copy in sends[k]:
             copy.wait_recv()
         x_low = jnp.where(me_x > 0, hx[k, 0], 0.0)
@@ -457,14 +432,8 @@
         v = inner + outer
         if k < POWERS - 1:
             sends.append(publish(k + 1, v))
-        if k < len(known):
-            pl.semaphore_wait(word.at[k], len(known[k]))
-
-    def padded(rows, start=0):
-        parts = [rows, jnp.zeros((LANES - start - rows.shape[0], LANES), F32)]
-        if start:
-            parts.insert(0, jnp.zeros((start, LANES), F32))
-        return jnp.concatenate(parts, axis=0)
+        if k == len(known) - 2:
+            hear(k + 1)
 
     class Pass:
         pass
@@ -473,7 +442,7 @@
 
     def solve_lead(number):
         p = passes[number]
-        p.r, w = eliminate(lead_4(number))
+        p.r, w = eliminate(finish_lead(number))
         p.w = padded(w)
         p.w_t = p.w.T
         p.l = None
@@ -483,7 +452,7 @@
 
     def solve_late(number, k):
         p = passes[number]
-        l_k, w_k = eliminate_row(late_4(number, k), p.w, p.w_t, k)
+        l_k, w_k = eliminate_row(finish_sum(number, k - LEAD + 1), p.w, p.w_t, k)
         l_k = padded(l_k, RHS * k)
         p.l = l_k if p.l is None else p.l + l_k
         if k < POWERS:
@@ -493,12 +462,12 @@
 
     def next_lead():
         u_ref[1] = apply_lead(0)
-        lead_0(1, gram_of(1))
+        start_lead(1)
 
     def next_late(k):
         q = solve_late(0, k)
         u_ref[1] = jnp.where(u_lane == k, q, u_ref[1])
-        late_0(1, k, gram_rows(1, k))
+        start_row(1, k)
 
     def factor_of(number):
         p = passes[number]
@@ -526,53 +495,47 @@
 
     last, before = POWERS, POWERS - 1
     add_column(last, v)
-    late_0(0, last, gram_rows(0, last))
-    lead_2(0)
-    late_1(0, last)
-    late_2(0, before)
-    lead_3(0)
-    late_2(0, last)
-    late_3(0, before)
+    start_row(0, last)
+    over_z(0, 0)
+    over_yx(0, 2)
+    over_z(0, 1)
+    over_z(0, 2)
+    share(0, 0)
     solve_lead(0)
     next_lead()
+    share(0, 1)
+    over_yx(1, 0)
     next_late(before)
-    late_3(0, last)
-    late_1(1, before)
-    lead_1(1)
+    share(0, 2)
+    over_yx(1, 1)
     next_late(last)
     first_r = factor_of(0)
-    late_1(1, last)
-    lead_2(1)
-    late_2(1, before)
-    late_2(1, last)
-    lead_3(1)
-    late_3(1, before)
+    over_yx(1, 2)
+    over_z(1, 0)
+    over_z(1, 1)
+    over_z(1, 2)
+    share(1, 0)
     solve_lead(1)
-    late_3(1, last)
+    give_lead()
+    share(1, 1)
     give_late(before)
+    share(1, 2)
     give_late(last)
     factor_ref[...] = dot_exact(factor_of(1)[:COLS], first_r)[:, :COLS]
-    give_lead()
 
     for copies in sends:
         for copy in copies:
             copy.wait_send()
     for number in range(2):
-        all_bytes(stage_a.at[number], n_g, asend.at[number, 0]).wait()
-        all_bytes(stage_b.at[number], ny, asend.at[number, 1]).wait()
-        all_bytes(stage_c.at[number], nz, asend.at[number, 2]).wait()
-        all_bytes(gathered.at[number], n_g, asend.at[number, 3]).wait()
-        for c in range(LATE):
+        for c in range(CHUNKS):
             to_partner(number, c, 0).wait_send()
-            all_bytes(late_yx.at[number, c], n_yx, lsend.at[number, c, 1]).wait()
-            all_bytes(late_z.at[number, c], nz, lsend.at[number, c, 2]).wait()
+            all_bytes(from_yx.at[number, c], n_yx, csend.at[number, c, 1]).wait()
+            all_bytes(from_z.at[number, c], nz, csend.at[number, c, 2]).wait()
             to_partner(number, c, 3).wait_send()
 
 
 def on_device(sizes, rhs, blocks):
     ny, nz, nc, nx = sizes
-    n_g = nx * nc
-    piece = 2 * RHS // n_g
     faces = blocks.transpose(0, 1, 3, 2, 4).reshape(14, 4, DOF * DOF)
     vmem = pltpu.VMEM
     basis, factor = pl.pallas_call(
@@ -592,27 +555,17 @@
             vmem((POWERS, 2, DOF, LANES), F32),
             vmem((POWERS, 2, DOF // 2, LANES), F32),
             vmem((2, ELEMS * DOF, LANES), F32),
-            vmem((2, n_g, piece, LANES), F32),
-            vmem((2, n_g, piece, LANES), F32),
-            vmem((2, ny, piece, LANES), F32),
-            vmem((2, nz, piece, LANES), F32),
-            vmem((2, piece, LANES), F32),
-            vmem((2, piece, LANES), F32),
-            vmem((2, piece, LANES), F32),
-            vmem((2, n_g, piece, LANES), F32),
-            vmem((2, LATE, 2, 8, LANES), F32),
-            vmem((2, LATE, 8, LANES), F32),
-            vmem((2, LATE, 3, 8, LANES), F32),
-            vmem((2, LATE, ny * nx, 8, LANES), F32),
-            vmem((2, LATE, nz, 8, LANES), F32),
-            vmem((2, LATE, 2, 8, LANES), F32),
+            vmem((2, CHUNKS, 2, 8, LANES), F32),
+            vmem((2, CHUNKS, 8, LANES), F32),
+            vmem((2, CHUNKS, 3, 8, LANES), F32),
+            vmem((2, CHUNKS, ny * nx, 8, LANES), F32),
+            vmem((2, CHUNKS, nz, 8, LANES), F32),
+            vmem((2, CHUNKS, 2, 8, LANES), F32),
             pltpu.SemaphoreType.DMA((1,)),
             pltpu.SemaphoreType.DMA((POWERS, 4)),
             pltpu.SemaphoreType.DMA((POWERS, 4)),
-            pltpu.SemaphoreType.DMA((2, 4)),
-            pltpu.SemaphoreType.DMA((2, 4)),
-            pltpu.SemaphoreType.DMA((2, LATE, 4)),
-            pltpu.SemaphoreType.DMA((2, LATE, 4)),
+            pltpu.SemaphoreType.DMA((2, CHUNKS, 4)),
+            pltpu.SemaphoreType.DMA((2, CHUNKS, 4)),
             pltpu.SemaphoreType.REGULAR((POWERS,)),
         ],
         compiler_params=pltpu.CompilerParams(

time: 80.7 us -> 77.1 us (0.955)
  Pallas kernels: 77.8 us -> 74.2 us
    pallas_call x1, Pallas kernels: 77.8 us -> 74.2 us  [on_device(): pl.pallas_call(functools.partial(kernel, sizes), out_shape=(jax.ShapeDtyp...]
where the time goes in v5:
time: 77.1 us; the launch traced here: 76.9 us
  Pallas kernels  74.2 us (96%)
  local copies, waits for them, and re-layouts  2.04 us (3%)
    pallas_call x1, Pallas kernels, on_device(): pl.pallas_call(functools.partial(kernel, sizes), out_shape=(jax.ShapeDtyp...  74.2 us
    unnamed x4, local copies, waits for them, and re-layouts  2.04 us

profile of v5, /device:TPU:1, one launch (start us, length us, event | category | flops | bytes accessed | tf_op | source)
XLA Modules:
  0.0 76.9 jit_solution(7450504590592698050)
XLA Ops:
  0.6 0.0 copy-start
  0.6 0.7 copy-done
  1.4 74.2 %krylov_qr.1 = (f32[5,2,4,1024]{3,2,1,0:T(4,128)S(1)}, f32[80,80]{1,0:T(8,128)S(1)}) custom-call(f32[2,4,1024]{2,1,0:T(4,128)S(1)} %bitcast.8, f32[14,4,4096]{2,1,0:T(4,128)} %bitcast.9), custom_call_target="tpu_custom_call" | custom-call | tf_op jit(solution)/shard_map/krylov_qr/pallas_call | solution.py:541
  75.6 0.7 copy.7
  76.2 0.6 copy.8
Async XLA Ops:
  0.6 0.8 copy-start

commit v6 on v5

--- a/solution.py
+++ b/solution.py
@@ -16,6 +16,7 @@
 PANEL = 16
 LEAD = 3
 CHUNKS = POWERS + 2 - LEAD
+SENT = (8, 4, 5)
 F32 = jnp.float32
 BF16 = jnp.bfloat16
 PAIRS = ((0, 5), (6, None), (1, 2), (3, 4))
@@ -154,9 +155,8 @@
     return lead + corner, jnp.where(at < start + PANEL, stacked(r), 0.0)
 
 
-def kernel(sizes, rhs_ref, blocks_ref, basis_ref, factor_ref, raw, b_f32, b_parts, vecs, ypack, hx, hy,
-           u_ref, halves, other_half, sums, from_yx, from_z, whole,
-           load_sem, hsend, hrecv, csend, crecv, word):
+def kernel(sizes, rhs_ref, blocks_ref, basis_ref, factor_ref, raw, b_f32, b_inner, b_y, b_x, vecs, ypack, hx, hy, u_ref,
+           load_sem, hsend, hrecv, csend, crecv, word, *chunks):
     ny, nz, nc, nx = sizes
     gx, gy = ny * nz * nc, nx
     me_x, me_y = lax.axis_index("gx"), lax.axis_index("gy")
@@ -237,7 +237,7 @@
     zero8 = jnp.zeros((8, LANES), F32)
     half8 = lane((8, LANES)) < 64
 
-    def prepare(places):
+    def prepare(places, parts_ref):
         @pl.loop(0, DOF // 8)
         def _(quad):
             for step in range(4):
@@ -258,8 +258,8 @@
         for i, place_ in enumerate(places):
             high, mid, low = split(b_f32[place_])
             for part, value in enumerate((mid, high, low)):
-                at = 2 * LANES * part + LANES * i
-                b_parts[places[0] // 2, :, at : at + LANES] = value
+                at = LANES * (len(places) * part + i)
+                parts_ref[:, at : at + LANES] = value
 
     v = transpose_groups(first)
     pl.semaphore_wait(barrier, count)
@@ -274,14 +274,16 @@
 
     tell(0)
     load.wait()
-    prepare((0, 1))
-    prepare((2, 3))
-
-    def product(which, vectors):
+    prepare((0, 1), b_inner)
+    prepare((3,), b_y)
+    prepare((2,), b_x)
+
+    def product(parts_ref, vectors):
         high, mid, low = split(jnp.concatenate(vectors, axis=0))
         both = jnp.concatenate([high, mid], axis=1)
-        wide = dot(b_parts[which, :, : 4 * LANES], jnp.concatenate([both, both], axis=0))
-        rest = dot(b_parts[which, :, 2 * LANES :], jnp.concatenate([low, high], axis=0))
+        width = parts_ref.shape[1] // 3
+        wide = dot(parts_ref[:, : 2 * width], jnp.concatenate([both, both], axis=0))
+        rest = dot(parts_ref[:, width:], jnp.concatenate([low, high], axis=0))
         total = wide[:, :LANES] + wide[:, LANES:] + rest
         out = total[:DOF]
         for e in range(1, ELEMS):
@@ -308,61 +310,91 @@
     def far_first(i, n):
         return lax.rem(n // 2 + (1 - 2 * lax.rem(i, 2)) * lax.div(i, 2), n)
 
+    halves, other_half, sums, from_yx, from_z, whole = (chunks[CHUNKS * i : CHUNKS * (i + 1)] for i in range(6))
+    row8, lane8 = row((8, LANES)), lane((8, LANES))
+
+    def turn_rows(rows, shifts):
+        out = rows
+        for i, shift in enumerate(shifts):
+            if shift % LANES:
+                out = jnp.where(row8 == i, pltpu.roll(rows, shift % LANES, 1), out)
+        return out
+
+    def pack(c, rows):
+        if SENT[c] == 8:
+            return rows
+        packed = jnp.where(lane8 < 64, rows, pltpu.roll(pltpu.roll(rows, 4, 0), 64, 1))[:4]
+        if SENT[c] == 4:
+            return packed
+        turned = turn_rows(rows, [64 + RHS * i for i in range(8)])
+        tail = jnp.sum(jnp.where(lane8 // RHS == row8, turned, 0.0), axis=0, keepdims=True)
+        return jnp.concatenate([packed, tail], axis=0)
+
+    def unpack(c, packed):
+        if SENT[c] == 8:
+            return packed
+        twice = jnp.concatenate([packed[:4], packed[:4]], axis=0)
+        rows = jnp.where(lane8 < 64, jnp.where(row8 < 4, twice, pltpu.roll(twice, 64, 1)), 0.0)
+        if SENT[c] == 4:
+            return rows
+        tail = jnp.where(lane8 // RHS == row8, jnp.broadcast_to(packed[4:], (8, LANES)), 0.0)
+        return rows + turn_rows(tail, [64 - RHS * i for i in range(8)])
+
     partner = place(at_y, at_z, nc - 1 - core, me_y)
 
     def to_partner(number, c, stage):
         if stage == 0:
-            src, dst = halves.at[number, c, nc - 1 - core], other_half.at[number, c]
+            src, dst = halves[c].at[number, nc - 1 - core], other_half[c].at[number]
         else:
-            src, dst = sums.at[number, c, 2], whole.at[number, c, core]
+            src, dst = sums[c].at[number, 2], whole[c].at[number, core]
         return remote(src, dst, csend.at[number, c, stage], crecv.at[number, c, stage], partner)
 
     def start_sum(number, c, rows):
-        halves[number, c, 0] = rows[:8]
-        halves[number, c, 1] = rows[8:]
+        halves[c][number, 0] = pack(c, rows[:8])
+        halves[c][number, 1] = pack(c, rows[8:])
         to_partner(number, c, 0).start()
 
     def over_yx(number, c):
         to_partner(number, c, 0).wait_recv()
-        total = halves[number, c, core] + other_half[number, c]
-        sums[number, c, 0] = total
+        total = halves[c][number, core] + other_half[c][number]
+        sums[c][number, 0] = total
 
         @pl.loop(0, n_yx - 1)
         def _(j):
             y = lax.rem(at_y + far_first(lax.div(j, nx) + 1, ny), ny)
             x = lax.rem(me_y + lax.rem(j, nx) + 1, nx)
             remote(
-                sums.at[number, c, 0], from_yx.at[number, c, me_yx],
+                sums[c].at[number, 0], from_yx[c].at[number, me_yx],
                 csend.at[number, c, 1], crecv.at[number, c, 1], place(y, at_z, core, x),
             ).start()
 
-        from_yx[number, c, me_yx] = total
+        from_yx[c][number, me_yx] = total
 
     def over_z(number, c):
-        all_bytes(from_yx.at[number, c], n_yx, crecv.at[number, c, 1]).wait()
-        total = add_up(from_yx.at[number, c], n_yx)
-        sums[number, c, 1] = total
+        all_bytes(from_yx[c].at[number], n_yx, crecv.at[number, c, 1]).wait()
+        total = add_up(from_yx[c].at[number], n_yx)
+        sums[c][number, 1] = total
 
         @pl.loop(1, nz)
         def _(i):
             other = lax.rem(at_z + far_first(i, nz), nz)
             remote(
-                sums.at[number, c, 1], from_z.at[number, c, at_z],
+                sums[c].at[number, 1], from_z[c].at[number, at_z],
                 csend.at[number, c, 2], crecv.at[number, c, 2], mate_z(other),
             ).start()
 
-        from_z[number, c, at_z] = total
+        from_z[c][number, at_z] = total
 
     def share(number, c):
-        all_bytes(from_z.at[number, c], nz, crecv.at[number, c, 2]).wait()
-        total = add_up(from_z.at[number, c], nz)
-        sums[number, c, 2] = total
+        all_bytes(from_z[c].at[number], nz, crecv.at[number, c, 2]).wait()
+        total = add_up(from_z[c].at[number], nz)
+        sums[c][number, 2] = total
         to_partner(number, c, 3).start()
-        whole[number, c, core] = total
+        whole[c][number, core] = total
 
     def finish_sum(number, c):
         to_partner(number, c, 3).wait_recv()
-        return jnp.concatenate([whole[number, c, 0], whole[number, c, 1]], axis=0)
+        return jnp.concatenate([unpack(c, whole[c][number, i]) for i in range(2)], axis=0)
 
     def gram_of(number):
         u = u_ref[number]
@@ -400,7 +432,7 @@
     for k in range(POWERS):
         z_low = jnp.where(at_cell == 0, 0.0, pltpu.roll(v, 16, 1))
         z_high = jnp.where(at_cell == 3, 0.0, pltpu.roll(v, LANES - 16, 1))
-        inner = v + product(0, [v, z_low, z_high, zero])
+        inner = v + product(b_inner, [v, z_low, z_high, zero])
         swapped = pltpu.roll(v, 64, 1)
         if k < len(known) - 1:
             hear(k)
@@ -415,10 +447,8 @@
             add_column(k, v)
             start_row(0, k)
             over_yx(0, 1)
-        for copy in sends[k]:
+        for copy in sends[k][2:]:
             copy.wait_recv()
-        x_low = jnp.where(me_x > 0, hx[k, 0], 0.0)
-        x_high = jnp.where(me_x < gx - 1, hx[k, 1], 0.0)
         y_low = jnp.where(me_y > 0, hy[k, 0], 0.0)
         y_high = jnp.where(me_y < gy - 1, hy[k, 1], 0.0)
         own_low, own_high = swapped[: DOF // 2], swapped[DOF // 2 :]
@@ -428,8 +458,12 @@
         y_high = jnp.concatenate(
             [jnp.where(half, own_low, pltpu.roll(y_high, 64, 1)), jnp.where(half, own_high, y_high)], axis=0
         )
-        outer = product(1, [x_low, x_high, y_low, y_high])
-        v = inner + outer
+        inner = inner + product(b_y, [y_low, y_high])
+        for copy in sends[k][:2]:
+            copy.wait_recv()
+        x_low = jnp.where(me_x > 0, hx[k, 0], 0.0)
+        x_high = jnp.where(me_x < gx - 1, hx[k, 1], 0.0)
+        v = inner + product(b_x, [x_low, x_high])
         if k < POWERS - 1:
             sends.append(publish(k + 1, v))
         if k == len(known) - 2:
@@ -529,50 +563,71 @@
     for number in range(2):
         for c in range(CHUNKS):
             to_partner(number, c, 0).wait_send()
-            all_bytes(from_yx.at[number, c], n_yx, csend.at[number, c, 1]).wait()
-            all_bytes(from_z.at[number, c], nz, csend.at[number, c, 2]).wait()
+            all_bytes(from_yx[c].at[number], n_yx, csend.at[number, c, 1]).wait()
+            all_bytes(from_z[c].at[number], nz, csend.at[number, c, 2]).wait()
             to_partner(number, c, 3).wait_send()
+
+
+def hand_over(basis_ref, factor_ref, basis_out, factor_out, sems):
+    copies = [
+        pltpu.make_async_copy(basis_ref, basis_out, sems.at[0]),
+        pltpu.make_async_copy(factor_ref, factor_out, sems.at[1]),
+    ]
+    for copy in copies:
+        copy.start()
+    for copy in copies:
+        copy.wait()
 
 
 def on_device(sizes, rhs, blocks):
     ny, nz, nc, nx = sizes
     faces = blocks.transpose(0, 1, 3, 2, 4).reshape(14, 4, DOF * DOF)
     vmem = pltpu.VMEM
+    shapes = (
+        jax.ShapeDtypeStruct((POWERS + 1, 2, 4, DOF * RHS), F32),
+        jax.ShapeDtypeStruct((COLS, COLS), F32),
+    )
     basis, factor = pl.pallas_call(
         functools.partial(kernel, sizes),
-        out_shape=(
-            jax.ShapeDtypeStruct((POWERS + 1, 2, 4, DOF * RHS), F32),
-            jax.ShapeDtypeStruct((COLS, COLS), F32),
-        ),
+        out_shape=shapes,
         in_specs=[pl.BlockSpec(memory_space=pltpu.VMEM), pl.BlockSpec(memory_space=pl.ANY)],
         out_specs=(pl.BlockSpec(memory_space=pltpu.VMEM),) * 2,
         scratch_shapes=[
             vmem((14, 4, DOF * DOF), F32),
             vmem((4, ELEMS * DOF, LANES), F32),
-            vmem((2, ELEMS * DOF, 6 * LANES), BF16),
+            vmem((ELEMS * DOF, 6 * LANES), BF16),
+            vmem((ELEMS * DOF, 3 * LANES), BF16),
+            vmem((ELEMS * DOF, 3 * LANES), BF16),
             vmem((POWERS + 1, DOF, LANES), F32),
             vmem((POWERS, 2, DOF // 2, LANES), F32),
             vmem((POWERS, 2, DOF, LANES), F32),
             vmem((POWERS, 2, DOF // 2, LANES), F32),
             vmem((2, ELEMS * DOF, LANES), F32),
-            vmem((2, CHUNKS, 2, 8, LANES), F32),
-            vmem((2, CHUNKS, 8, LANES), F32),
-            vmem((2, CHUNKS, 3, 8, LANES), F32),
-            vmem((2, CHUNKS, ny * nx, 8, LANES), F32),
-            vmem((2, CHUNKS, nz, 8, LANES), F32),
-            vmem((2, CHUNKS, 2, 8, LANES), F32),
             pltpu.SemaphoreType.DMA((1,)),
             pltpu.SemaphoreType.DMA((POWERS, 4)),
             pltpu.SemaphoreType.DMA((POWERS, 4)),
             pltpu.SemaphoreType.DMA((2, CHUNKS, 4)),
             pltpu.SemaphoreType.DMA((2, CHUNKS, 4)),
             pltpu.SemaphoreType.REGULAR((POWERS,)),
+        ]
+        + [
+            vmem(shape + (rows, LANES), F32)
+            for shape in ((2, 2), (2,), (2, 3), (2, ny * nx), (2, nz), (2, 2))
+            for rows in SENT
         ],
         compiler_params=pltpu.CompilerParams(
             collective_id=0, has_side_effects=True, vmem_limit_bytes=53 * 1024 * 1024 + 256 * 1024
         ),
         name="krylov_qr",
     )(rhs.reshape(2, 4, DOF * RHS), faces)
+    basis, factor = pl.pallas_call(
+        hand_over,
+        out_shape=shapes,
+        in_specs=[pl.BlockSpec(memory_space=pltpu.VMEM)] * 2,
+        out_specs=(pl.BlockSpec(memory_space=pl.ANY),) * 2,
+        scratch_shapes=[pltpu.SemaphoreType.DMA((2,))],
+        name="hand_over",
+    )(basis, factor)
     return basis.reshape(POWERS + 1, 1, 2, 4, DOF * RHS), factor
 
 

time: 77.1 us -> 78.1 us (1.013)
  Pallas kernels: 74.2 us -> 75.2 us
    pallas_call x1 -> x2, Pallas kernels: 74.2 us -> 75.2 us  [the longest x1 73.6 us: on_device(): pl.pallas_call(functools.partial(kernel, sizes), out_shape=shapes, in_spe...]
    unnamed x4 -> x6, local copies, waits for them, and re-layouts: 2.04 us -> 2.01 us
where the time goes in v6:
time: 78.1 us; the launch traced here: 77.9 us
  Pallas kernels  75.2 us (96%)
  local copies, waits for them, and re-layouts  2.01 us (3%)
    pallas_call x1, Pallas kernels, on_device(): pl.pallas_call(functools.partial(kernel, sizes), out_shape=shapes, in_spe...  73.6 us
    unnamed x6, local copies, waits for them, and re-layouts  2.01 us
    pallas_call x1, Pallas kernels, on_device(): pl.pallas_call(hand_over, out_shape=shapes, in_specs=[pl.BlockSpec(memory...  1.6 us

profile of v6, /device:TPU:1, one launch (start us, length us, event | category | flops | bytes accessed | tf_op | source)
XLA Modules:
  0.0 77.9 jit_solution(9145949299258833018)
XLA Ops:
  0.6 0.0 copy-start.2
  0.6 0.7 copy-done.2
  1.4 73.6 %krylov_qr.1 = (f32[5,2,4,1024]{3,2,1,0:T(4,128)S(1)}, f32[80,80]{1,0:T(8,128)S(1)}) custom-call(f32[2,4,1024]{2,1,0:T(4,128)S(1)} %bitcast.7, f32[14,4,4096]{2,1,0:T(4,128)} %bitcast.8), custom_call_target="tpu_custom_call" | custom-call | tf_op jit(solution)/shard_map/krylov_qr/pallas_call | solution.py:590
  75.0 0.0 copy-start
  75.0 0.6 copy-done
  75.7 0.0 copy-start.1
  75.7 0.6 copy-done.1
  76.3 1.6 %hand_over.1 = (f32[5,2,4,1024]{3,2,1,0:T(4,128)}, f32[80,80]{1,0:T(8,128)}) custom-call(f32[5,2,4,1024]{3,2,1,0:T(4,128)} %copy-done, f32[80,80]{1,0:T(8,128)} %copy-done.1), custom_call_target="tpu_custom_call" | custom-call | tf_op jit(solution)/shard_map/hand_over/pallas_call | solution.py:623
Async XLA Ops:
  0.6 0.8 copy-start.2
  75.0 0.7 copy-start
  75.7 0.6 copy-start.1

commit v7 on v6

--- a/solution.py
+++ b/solution.py
@@ -419,6 +419,12 @@
 
     def start_row(number, k):
         start_sum(number, k - LEAD + 1, gram_of(number)[RHS * k : RHS * (k + 1)])
+
+    def of_elements(q):
+        column = q[:DOF]
+        for e in range(1, ELEMS):
+            column = jnp.where(lanes // RHS == e, q[DOF * e : DOF * (e + 1)], column)
+        return column
 
     u_lane = lane((ELEMS * DOF, LANES)) // RHS
 
@@ -521,11 +527,7 @@
             give(k, columns[k])
 
     def give_late(k):
-        q = solve_late(1, k)
-        column = q[:DOF]
-        for e in range(1, ELEMS):
-            column = jnp.where(lanes // RHS == e, q[DOF * e : DOF * (e + 1)], column)
-        give(k, column)
+        give(k, of_elements(solve_late(1, k)))
 
     last, before = POWERS, POWERS - 1
     add_column(last, v)
@@ -533,8 +535,8 @@
     over_z(0, 0)
     over_yx(0, 2)
     over_z(0, 1)
+    share(0, 0)
     over_z(0, 2)
-    share(0, 0)
     solve_lead(0)
     next_lead()
     share(0, 1)
@@ -543,16 +545,16 @@
     share(0, 2)
     over_yx(1, 1)
     next_late(last)
+    over_z(1, 0)
+    over_yx(1, 2)
     first_r = factor_of(0)
-    over_yx(1, 2)
-    over_z(1, 0)
     over_z(1, 1)
     over_z(1, 2)
     share(1, 0)
     solve_lead(1)
-    give_lead()
     share(1, 1)
     give_late(before)
+    give_lead()
     share(1, 2)
     give_late(last)
     factor_ref[...] = dot_exact(factor_of(1)[:COLS], first_r)[:, :COLS]
@@ -566,17 +568,6 @@
             all_bytes(from_yx[c].at[number], n_yx, csend.at[number, c, 1]).wait()
             all_bytes(from_z[c].at[number], nz, csend.at[number, c, 2]).wait()
             to_partner(number, c, 3).wait_send()
-
-
-def hand_over(basis_ref, factor_ref, basis_out, factor_out, sems):
-    copies = [
-        pltpu.make_async_copy(basis_ref, basis_out, sems.at[0]),
-        pltpu.make_async_copy(factor_ref, factor_out, sems.at[1]),
-    ]
-    for copy in copies:
-        copy.start()
-    for copy in copies:
-        copy.wait()
 
 
 def on_device(sizes, rhs, blocks):
@@ -620,14 +611,6 @@
         ),
         name="krylov_qr",
     )(rhs.reshape(2, 4, DOF * RHS), faces)
-    basis, factor = pl.pallas_call(
-        hand_over,
-        out_shape=shapes,
-        in_specs=[pl.BlockSpec(memory_space=pltpu.VMEM)] * 2,
-        out_specs=(pl.BlockSpec(memory_space=pl.ANY),) * 2,
-        scratch_shapes=[pltpu.SemaphoreType.DMA((2,))],
-        name="hand_over",
-    )(basis, factor)
     return basis.reshape(POWERS + 1, 1, 2, 4, DOF * RHS), factor
 
 

time: 78.1 us -> 76.1 us (0.974)
  Pallas kernels: 75.2 us -> 73.2 us
    pallas_call x1 -> x0, Pallas kernels: 1.6 us -> none  [on_device(): pl.pallas_call(hand_over, out_shape=shapes, in_specs=[pl.BlockSpec(memory...]
    unnamed x6 -> x4, local copies, waits for them, and re-layouts: 2.01 us -> 2.04 us
where the time goes in v7:
time: 76.1 us; the launch traced here: 75.9 us
  Pallas kernels  73.2 us (96%)
  local copies, waits for them, and re-layouts  2.04 us (3%)
    pallas_call x1, Pallas kernels, on_device(): pl.pallas_call(functools.partial(kernel, sizes), out_shape=shapes, in_spe...  73.2 us
    unnamed x4, local copies, waits for them, and re-layouts  2.04 us

profile of v7, /device:TPU:1, one launch (start us, length us, event | category | flops | bytes accessed | tf_op | source)
XLA Modules:
  0.0 75.9 jit_solution(12909862269191521460)
XLA Ops:
  0.6 0.0 copy-start
  0.6 0.7 copy-done
  1.4 73.2 %krylov_qr.1 = (f32[5,2,4,1024]{3,2,1,0:T(4,128)S(1)}, f32[80,80]{1,0:T(8,128)S(1)}) custom-call(f32[2,4,1024]{2,1,0:T(4,128)S(1)} %bitcast.8, f32[14,4,4096]{2,1,0:T(4,128)} %bitcast.9), custom_call_target="tpu_custom_call" | custom-call | tf_op jit(solution)/shard_map/krylov_qr/pallas_call | solution.py:581
  74.6 0.7 copy.7
  75.3 0.6 copy.8
Async XLA Ops:
  0.6 0.8 copy-start
